TPU v7x, 256 devices: a whole 4x4x8 slice. The times are simulated.
256 devices in a mesh: gx: 8 (over z), gz: 8 (over x, core), gy: 4 (over y).
Axes of the slice: x: 4, y: 4, z: 8, core: 2. Of those that a mesh axis runs over, the one named last changes fastest.
Arguments:
- velocity: float32 [3, 512, 512, 512], P(None, ('gx', 'gz'), None, 'gy'), may hold values from -5 to 5, as said below
- spacing: float32 [513], replicated, may hold values from 0.15 to 3.4, as said below
Outputs:
- pressure: float32 [512, 512, 512], P(('gx', 'gz'), None, 'gy')
Inputs may be any that keep to these rules, and one draw needn't show every extreme that they name: `velocity`: velocity components at the grid nodes. `spacing`: entry 0 is the gap from the lower wall to the first node and entry 512 the gap from the last node to the upper wall.
All inputs are finite; a program needn't handle non-finite values.
Results may differ from a plain program's by a relative error of at most 0.0003.
Values sent between devices are 32-bit elements; how exact they have to be, the bound alone decides.
No kernel may reach another device: no remote copies, remote signals or barrier semaphores. Data moves between devices by JAX's collectives and lax.ppermute only.
A program may use at most 64 MiB of HBM per device.

v0:
```python
import functools
import math

import jax
import jax.numpy as jnp
import ml_dtypes
import numpy as np
from jax import lax
from jax.experimental import pallas as pl
from jax.experimental.pallas import tpu as pltpu
from jax.sharding import PartitionSpec as P

span_step = 0.5
f32 = jnp.float32
bf16 = jnp.bfloat16


def np_tables(length, step_size):
    index = np.arange(length)
    wave = np.where(index == 1, length // 2, index // 2)
    phase = (index[:, None] * wave[None, :]) % length
    angle = 2.0 * math.pi / length * phase
    odd_high = np.logical_and(index % 2 == 1, index >= 3)[None, :]
    forward = np.where(odd_high, -np.sin(angle), np.cos(angle))
    kappa = 2.0 * math.pi / (length * step_size) * wave
    scale = np.where(index >= 2, kappa, 0.0)[None, :]
    derive = np.where(odd_high, np.cos(angle), np.sin(angle)) * scale
    weight = np.where(index >= 2, 2.0, 1.0) / length
    inverse = (forward * weight[None, :]).T
    return forward, derive, inverse, (kappa * kappa).astype(np.float32)


def split_np(table):
    high = table.astype(np.float32).astype(ml_dtypes.bfloat16)
    low = (table - high.astype(np.float64)).astype(np.float32).astype(ml_dtypes.bfloat16)
    return high, low


def left_table(table):
    high, low = split_np(table)
    return np.concatenate([high, low, high], axis=1)


def right_table(table):
    high, low = split_np(table)
    return np.concatenate([high, low, high], axis=0)


def parts(x, axis):
    high = x.astype(bf16)
    low = (x - high.astype(f32)).astype(bf16)
    return jnp.concatenate([high, high, low], axis=axis)


def params(mib):
    return pltpu.CompilerParams(vmem_limit_bytes=mib * 1024 * 1024)


def cost(flops, size):
    return pl.CostEstimate(flops=flops, bytes_accessed=size, transcendentals=0)


def span_field_kernel(w_ref, t_ref, o_ref):
    x = jnp.concatenate([w_ref[0, 0], w_ref[0, 1]], axis=1)
    y = jnp.dot(t_ref[...], parts(x, 0), preferred_element_type=f32)
    for p in range(2):
        part = y[:, 128 * p : 128 * (p + 1)]
        o_ref[:, p] = part.reshape(part.shape[0] // 8, 8, 128)


def flow_field_kernel(u_ref, v_ref, before_ref, after_ref, width_ref, t_ref, o_ref):
    step = pl.program_id(0)
    lane = lax.broadcasted_iota(jnp.int32, v_ref.shape[2:], 1)
    width = width_ref[...]
    slopes = []
    for p in range(2):
        v = v_ref[0, p]
        z = step * 2 + p
        before = jnp.transpose(jnp.broadcast_to(before_ref[pl.ds(z, 1), :], (128, v.shape[0])))
        after = jnp.transpose(jnp.broadcast_to(after_ref[pl.ds(z, 1), :], (128, v.shape[0])))
        down = jnp.where(lane == 0, before, pltpu.roll(v, 1, 1))
        up = jnp.where(lane == 127, after, pltpu.roll(v, 127, 1))
        slopes.append((up - down) / width)
    u = jnp.concatenate([u_ref[0, 0], u_ref[0, 1]], axis=1)
    s = jnp.concatenate(slopes, axis=1)
    x = jnp.concatenate([parts(u, 0), parts(s, 0)], axis=0)
    y = jnp.dot(t_ref[...], x, preferred_element_type=f32)
    for p in range(2):
        part = y[:, 128 * p : 128 * (p + 1)]
        o_ref[:, p] = part.reshape(part.shape[0] // 8, 8, 128)


def factor_kernel(low_ref, up_ref, sigma_ref, inv_ref, m_ref, r_ref, v_ref, w_ref, ends_ref):
    rows = inv_ref.shape[0]
    tiles = inv_ref.shape[1]

    def ahead(y, carry):
        low = low_ref[y]
        up = up_ref[y]
        out = []
        for t in range(tiles):
            r, val = carry[t]
            pivot = -(low + up) - sigma_ref[t] - low * r
            inv = 1.0 / pivot
            r = up * inv
            m = low * inv
            val = -m * val
            inv_ref[y, t] = inv
            m_ref[y, t] = m
            r_ref[y, t] = r
            v_ref[t, pl.ds(y, 8, stride=rows), :] = val
            out.append((r, val))
        return tuple(out)

    zero = jnp.zeros((8, 128), f32)
    one = jnp.ones((8, 128), f32)
    lax.fori_loop(0, rows, ahead, ((zero, one),) * tiles)

    def back(s, carry):
        y = rows - 1 - s
        out = []
        for t in range(tiles):
            v, w = carry[t]
            r = r_ref[y, t]
            v = v_ref[t, pl.ds(y, 8, stride=rows), :] - r * v
            w = -r * w
            v_ref[t, pl.ds(y, 8, stride=rows), :] = v
            w_ref[t, pl.ds(y, 8, stride=rows), :] = w
            out.append((v, w))
        return tuple(out)

    first = lax.fori_loop(0, rows, back, ((zero, one),) * tiles)
    for t in range(tiles):
        ends_ref[0, t] = first[t][0]
        ends_ref[1, t] = v_ref[t, pl.ds(rows - 1, 8, stride=rows), :]
        ends_ref[2, t] = first[t][1]
        ends_ref[3, t] = w_ref[t, pl.ds(rows - 1, 8, stride=rows), :]


def span_modes(x_ref, t_ref, mode):
    planes = x_ref.shape[0] // 8
    both = [
        jnp.transpose(x_ref[pl.ds(mode + p, planes, stride=8), :]) for p in range(2)
    ]
    x = jnp.concatenate(both, axis=0)
    return jnp.dot(parts(x, 1), t_ref[...], preferred_element_type=f32)


def span_first_kernel(x_ref, t_ref, o_ref):
    tiles = o_ref.shape[0]
    for mode in range(0, 8, 2):
        y = span_modes(x_ref, t_ref, mode)
        for t in range(tiles):
            o_ref[t, mode * 128 : (mode + 2) * 128, :] = y[:, t * 128 : (t + 1) * 128]


def sweep_kernel(x_ref, s_ref, t_ref, inv_ref, m_ref, r_ref, o_ref, ends_ref):
    tiles = o_ref.shape[0]
    rows = inv_ref.shape[0]
    for mode in range(0, 8, 2):
        y = span_modes(x_ref, t_ref, mode)
        part = slice(mode * 128, (mode + 2) * 128)
        for t in range(tiles):
            o_ref[t, part, :] = y[:, t * 128 : (t + 1) * 128] + s_ref[t, part, :]

    def ahead(y, carry):
        out = []
        for t in range(tiles):
            side = o_ref[t, pl.ds(y, 8, stride=rows), :]
            val = side * inv_ref[y, t] - m_ref[y, t] * carry[t]
            o_ref[t, pl.ds(y, 8, stride=rows), :] = val
            out.append(val)
        return tuple(out)

    zero = jnp.zeros((8, 128), f32)
    lax.fori_loop(0, rows, ahead, (zero,) * tiles, unroll=4)

    def back(s, carry):
        y = rows - 1 - s
        out = []
        for t in range(tiles):
            val = o_ref[t, pl.ds(y, 8, stride=rows), :] - r_ref[y, t] * carry[t]
            o_ref[t, pl.ds(y, 8, stride=rows), :] = val
            out.append(val)
        return tuple(out)

    first = lax.fori_loop(0, rows, back, (zero,) * tiles, unroll=4)
    for t in range(tiles):
        ends_ref[0, t] = first[t]
        ends_ref[1, t] = o_ref[t, pl.ds(rows - 1, 8, stride=rows), :]


def join_kernel(me_ref, y_ref, v_ref, w_ref, ys_ref, vw_ref, t_ref, o_ref, b_ref, f_ref):
    blocks = vw_ref.shape[0]
    tiles = y_ref.shape[0]
    me = me_ref[0]
    for t in range(tiles):
        alpha = jnp.zeros((8, 128), f32)
        beta = jnp.zeros((8, 128), f32)
        alphas, betas, starts, scales = [], [], [], []
        for g in range(blocks):
            slot = lax.rem(me + blocks - g, blocks)
            yf = ys_ref[slot, 0, t]
            yb = ys_ref[slot, 1, t]
            vf, vb, wf, wb = (vw_ref[g, n, t] for n in range(4))
            scale = 1.0 / (1.0 - vf * beta)
            start = (yf + vf * alpha) * scale
            starts.append(start)
            scales.append(wf * scale)
            alpha, beta = (
                yb + vb * (alpha + beta * start),
                wb + vb * beta * wf * scale,
            )
            alphas.append(alpha)
            betas.append(beta)
        after = jnp.zeros((8, 128), f32)
        f_ref[blocks, t] = after
        b_ref[0, t] = after
        for g in range(blocks - 1, -1, -1):
            b_ref[g + 1, t] = alphas[g] + betas[g] * after
            after = starts[g] + scales[g] * after
            f_ref[g, t] = after
    for mode in range(0, 8, 2):
        columns = []
        for t in range(tiles):
            both = []
            for p in range(2):
                part = slice((mode + p) * 128, (mode + p + 1) * 128)
                left = b_ref[me, t, pl.ds(mode + p, 1), :]
                right = f_ref[me + 1, t, pl.ds(mode + p, 1), :]
                both.append(y_ref[t, part, :] + v_ref[t, part, :] * left + w_ref[t, part, :] * right)
            columns.append(jnp.concatenate(both, axis=0))
        x = jnp.concatenate(columns, axis=1)
        y = lax.dot_general(
            t_ref[...], parts(x, 1), (((1,), (1,)), ((), ())), preferred_element_type=f32
        )
        for p in range(2):
            part = y[:, 128 * p : 128 * (p + 1)]
            o_ref[:, mode + p] = part.reshape(part.shape[0] // 8, 8, 128)


def flow_inverse_kernel(x_ref, t_ref, o_ref):
    slots = x_ref.shape[0] // 8
    for plane in range(0, 8, 2):
        x = jnp.concatenate(
            [x_ref[pl.ds(plane + p, slots, stride=8), :] for p in range(2)], axis=1
        )
        y = jnp.dot(t_ref[...], parts(x, 0), preferred_element_type=f32)
        for p in range(2):
            o_ref[plane + p] = y[:, 128 * p : 128 * (p + 1)]


def local(velocity, spacing):
    planes, flow_length, rows = velocity.shape[1:]
    size_x = lax.axis_size("gx")
    size_z = lax.axis_size("gz")
    blocks = lax.axis_size("gy")
    group = size_x * size_z
    span_length = planes * group
    modes = flow_length // group
    tiles = span_length // 128
    flow_forward, flow_derive, flow_inverse, flow_square = np_tables(flow_length, 1.0)
    span_forward, span_derive, span_inverse, span_square = np_tables(span_length, span_step)
    field_flops = 2 * 3 * planes * rows * flow_length * flow_length
    field_bytes = 4 * planes * rows * flow_length
    me = lax.axis_index("gy")
    both = ("gx", "gz")

    def moved(x):
        return lax.all_to_all(x, both, split_axis=0, concat_axis=0, tiled=True)

    field_shape = jax.ShapeDtypeStruct((group, planes, modes, rows), f32)
    table = jnp.asarray(left_table(flow_forward.T))
    plane_block = lambda c: pl.BlockSpec((1, 2, flow_length, rows), lambda i: (c, i, 0, 0))
    whole = lambda *shape: pl.BlockSpec(shape, lambda i: (0,) * len(shape))
    out_block = pl.BlockSpec((group, 2, modes, rows), lambda i: (0, i, 0, 0))
    span_sent = pl.pallas_call(
        span_field_kernel,
        grid=(planes // 2,),
        in_specs=[plane_block(2), whole(*table.shape)],
        out_specs=out_block,
        out_shape=field_shape,
        compiler_params=params(32),
        cost_estimate=cost(field_flops, 2 * field_bytes),
        name="span_field",
    )(velocity, table)
    span_here = moved(span_sent)

    v = velocity[1]
    up = [(i, i + 1) for i in range(blocks - 1)]
    down = [(j, i) for i, j in up]
    before = lax.ppermute(v[:, :, rows - 1], "gy", up)
    after = lax.ppermute(v[:, :, 0], "gy", down)
    gaps = lax.dynamic_slice_in_dim(spacing, me * rows, rows + 1)
    width = gaps[:-1] + gaps[1:]
    lower = 2.0 / (width * gaps[:-1])
    upper = 2.0 / (width * gaps[1:])
    flow_table = jnp.asarray(
        np.concatenate([left_table(flow_derive.T), left_table(flow_forward.T)], axis=1)
    )
    flow_sent = pl.pallas_call(
        flow_field_kernel,
        grid=(planes // 2,),
        in_specs=[
            plane_block(0),
            plane_block(1),
            whole(planes, flow_length),
            whole(planes, flow_length),
            whole(1, rows),
            whole(*flow_table.shape),
        ],
        out_specs=out_block,
        out_shape=field_shape,
        compiler_params=params(40),
        cost_estimate=cost(2 * field_flops, 3 * field_bytes),
        name="flow_field",
    )(velocity, velocity, before, after, width.reshape(1, rows), flow_table)
    flow_here = moved(flow_sent)

    first_mode = (lax.axis_index("gx") * size_z + lax.axis_index("gz")) * modes
    mode_square = lax.dynamic_slice_in_dim(jnp.asarray(flow_square), first_mode, modes)
    sigma = mode_square[None, :, None] + jnp.asarray(span_square).reshape(tiles, 1, 128)
    step_shape = jax.ShapeDtypeStruct((rows, tiles, modes, 128), f32)
    slab_shape = jax.ShapeDtypeStruct((tiles, modes * rows, 128), f32)
    vmem = pl.BlockSpec(memory_space=pltpu.VMEM)
    smem = pl.BlockSpec(memory_space=pltpu.SMEM)
    inv, m, r, v_all, w_all, vw_ends = pl.pallas_call(
        factor_kernel,
        in_specs=[smem, smem, vmem],
        out_specs=[vmem] * 6,
        out_shape=[step_shape] * 3
        + [slab_shape] * 2
        + [jax.ShapeDtypeStruct((4, tiles, modes, 128), f32)],
        compiler_params=params(32),
        cost_estimate=cost(field_flops, 5 * field_bytes),
        name="factor",
    )(lower, upper, sigma)
    vw = lax.all_gather(vw_ends, "gy", axis=0, tiled=False)

    flat = (span_length * modes, rows)
    span_source = pl.pallas_call(
        span_first_kernel,
        in_specs=[vmem, vmem],
        out_specs=vmem,
        out_shape=slab_shape,
        compiler_params=params(32),
        cost_estimate=cost(field_flops, 2 * field_bytes),
        name="span_first",
    )(span_here.reshape(flat), jnp.asarray(right_table(span_derive)))
    y_all, y_ends = pl.pallas_call(
        sweep_kernel,
        in_specs=[vmem] * 6,
        out_specs=[vmem] * 2,
        out_shape=[slab_shape, jax.ShapeDtypeStruct((2, tiles, modes, 128), f32)],
        compiler_params=params(40),
        cost_estimate=cost(field_flops, 6 * field_bytes),
        name="sweep",
    )(flow_here.reshape(flat), span_source, jnp.asarray(right_table(span_forward)), inv, m, r)
    shifted = [y_ends] + [
        lax.ppermute(y_ends, "gy", [(i, (i + s) % blocks) for i in range(blocks)])
        for s in range(1, blocks)
    ]
    ys = jnp.stack(shifted)
    end_shape = (blocks + 1, tiles, modes, 128)
    back_sent = pl.pallas_call(
        join_kernel,
        in_specs=[smem] + [vmem] * 6,
        out_specs=vmem,
        out_shape=jax.ShapeDtypeStruct((group, modes, planes, rows), f32),
        scratch_shapes=[pltpu.VMEM(end_shape, f32), pltpu.VMEM(end_shape, f32)],
        compiler_params=params(40),
        cost_estimate=cost(field_flops, 4 * field_bytes),
        name="join",
    )(
        me.reshape(1).astype(jnp.int32),
        y_all,
        v_all,
        w_all,
        ys,
        vw,
        jnp.asarray(left_table(span_inverse.T)),
    )
    back_here = moved(back_sent)
    return pl.pallas_call(
        flow_inverse_kernel,
        in_specs=[vmem, vmem],
        out_specs=vmem,
        out_shape=jax.ShapeDtypeStruct((planes, flow_length, rows), f32),
        compiler_params=params(32),
        cost_estimate=cost(field_flops, 2 * field_bytes),
        name="flow_inverse",
    )(back_here.reshape(flow_length * planes, rows), jnp.asarray(left_table(flow_inverse.T)))


def solution(mesh):
    return jax.shard_map(
        local,
        mesh=mesh,
        in_specs=(P(None, ("gx", "gz"), None, "gy"), P()),
        out_specs=P(("gx", "gz"), None, "gy"),
        check_vma=False,
    )
```

profile of v0, /device:TPU:8, one launch (start us, length us, event | category | flops | bytes accessed | tf_op | source)
XLA Modules:
  0.0 222.5 jit_solution(7614015364957330358)
XLA Ops:
  0.0 2.8 %copy-done = f32[3,8,512,128]{3,2,1,0:T(8,128)S(1)} copy-done((f32[3,8,512,128]{3,2,1,0:T(8,128)S(1)}, f32[3,8,512,128]{3,2,1,0:T(8,128)}, u32[]{:S(2)}) %copy-start) | copy-done | bytes 6291480
  2.8 1.4 copy-done.15
  4.2 3.5 %span_field.1 = f32[64,8,8,128]{3,2,1,0:T(8,128)} custom-call(f32[3,8,512,128]{3,2,1,0:T(8,128)S(1)} %copy-done, bf16[512,1536]{1,0:T(8,128)(2,1)S(1)} %copy-done.15), custom_call_target="tpu_custom_call" | custom-call | flops 1610612736 | bytes 4194304 | tf_op jit(solution)/shard_map/span_field/pallas_call | solution.py:277
  7.7 12.2 %all-to-all-start.1 = ((f32[64,8,8,128]{3,2,1,0:T(8,128)}), f32[64,8,8,128]{3,2,1,0:T(8,128)}, u32[]{:S(2)}, u32[]{:S(2)}) async-start(f32[64,8,8,128]{3,2,1,0:T(8,128)} %span_field.1), calls=%async_computation.1 | async-start | bytes 4194304 | tf_op jit(solution)/shard_map/all_to_all | solution.py:270
  19.9 1.6 slice-done
  21.5 2.0 copy.13
  24.2 2.3 %collective-permute-start.1 = (f32[8,512]{1,0:T(8,128)S(1)}, f32[8,512]{1,0:T(8,128)S(1)}, u32[]{:S(2)}, u32[]{:S(2)}) collective-permute-start(f32[8,512]{1,0:T(8,128)S(1)} %get-tuple-element.21), channel_id=1, source_target_pairs={{1,0},{2,1},{3,2},{5,4},{6,5},{7,6},{9,8},{10,9},{11,10},{13,12},{... | collective-permute-start | bytes 49160 | tf_op jit(solution)/shard_map/ppermute | solution.py:293
  26.5 3.5 %collective-permute-start = (f32[8,512]{1,0:T(8,128)S(1)}, f32[8,512]{1,0:T(8,128)S(1)}, u32[]{:S(2)}, u32[]{:S(2)}) collective-permute-start(f32[8,512]{1,0:T(8,128)S(1)} %get-tuple-element.22), channel_id=1, source_target_pairs={{0,1},{1,2},{2,3},{4,5},{5,6},{6,7},{8,9},{9,10},{10,11},{12,13},{... | collective-permute-start | bytes 49160 | tf_op jit(solution)/shard_map/ppermute | solution.py:292
  32.1 2.8 %copy-done.1 = f32[3,8,512,128]{3,2,1,0:T(8,128)S(1)} copy-done((f32[3,8,512,128]{3,2,1,0:T(8,128)S(1)}, f32[3,8,512,128]{3,2,1,0:T(8,128)}, u32[]{:S(2)}) %copy-start.1) | copy-done | bytes 6291480
  34.9 1.9 copy-done.2
  36.8 6.6 %flow_field.1 = f32[64,8,8,128]{3,2,1,0:T(8,128)} custom-call(f32[3,8,512,128]{3,2,1,0:T(8,128)S(1)} %copy-done.1, f32[3,8,512,128]{3,2,1,0:T(8,128)S(1)} %copy-done.1, f32[8,512]{1,0:T(8,128)S(1)} %collective-permute-done.before_ref, f32[8,512]{1,0:T(8,128)S(1)} %collective-permute-done.1.after_ref, f32[1,128]{1,0:T(1,128)S(1)} %get-tuple-element.24.width_ref, ...), custom_call_target="tpu_custom_call" | custom-call | flops 3221225472 | bytes 6291456 | tf_op jit(solution)/shard_map/flow_field/pallas_call | solution.py:301
  43.4 27.7 %all-to-all-done.1 = f32[64,8,8,128]{3,2,1,0:T(8,128)} async-done(((f32[64,8,8,128]{3,2,1,0:T(8,128)}), f32[64,8,8,128]{3,2,1,0:T(8,128)}, u32[]{:S(2)}, u32[]{:S(2)}) %all-to-all-start.1) | async-done | bytes 2097184 | tf_op jit(solution)/shard_map/all_to_all | solution.py:270
  71.1 5.3 %all-to-all-start = ((f32[64,8,8,128]{3,2,1,0:T(8,128)}), f32[64,8,8,128]{3,2,1,0:T(8,128)S(1)}, u32[]{:S(2)}, u32[]{:S(2)}) async-start(f32[64,8,8,128]{3,2,1,0:T(8,128)} %flow_field.1), calls=%async_computation | async-start | bytes 4194304 | tf_op jit(solution)/shard_map/all_to_all | solution.py:270
  77.3 10.4 %factor.1 = (f32[128,4,8,128]{3,2,1,0:T(8,128)S(1)}, f32[128,4,8,128]{3,2,1,0:T(8,128)S(1)}, f32[128,4,8,128]{3,2,1,0:T(8,128)S(1)}, f32[4,1024,128]{2,1,0:T(8,1...) custom-call(f32[128]{0:T(128)S(1)} %get-tuple-element.25.low_ref, f32[128]{0:T(128)S(1)} %get-tuple-element.23.up_ref, ...), custom_call_target="tpu_custom_call" | custom-call | flops 1610612736 | bytes 10485760 | tf_op jit(solution)/shard_map/factor/pallas_call | solution.py:327
  90.4 1.4 copy-done.7
  91.8 1.4 copy-done.9
  93.1 1.4 copy-done.11
  94.5 3.4 %span_first.1.s_ref = f32[4,1024,128]{2,1,0:T(8,128)S(1)} custom-call(f32[4096,128]{1,0:T(8,128)} %bitcast.6.x_ref, bf16[1536,512]{1,0:T(8,128)(2,1)S(1)} %copy-done.18), custom_call_target="tpu_custom_call" | custom-call | flops 1610612736 | bytes 4194304 | tf_op jit(solution)/shard_map/span_first/pallas_call | solution.py:341
  97.9 1.4 copy-done.13
  99.3 28.5 %all-to-all-done = f32[64,8,8,128]{3,2,1,0:T(8,128)S(1)} async-done(((f32[64,8,8,128]{3,2,1,0:T(8,128)}), f32[64,8,8,128]{3,2,1,0:T(8,128)S(1)}, u32[]{:S(2)}, u32[]{:S(2)}) %all-to-all-start) | async-done | bytes 2097184 | tf_op jit(solution)/shard_map/all_to_all | solution.py:270
  127.8 1.6 copy-done.8
  129.4 1.6 copy-done.10
  131.0 1.6 copy-done.12
  132.5 1.6 copy-done.14
  134.1 1.4 copy-done.17
  135.6 8.5 %sweep.1 = (f32[4,1024,128]{2,1,0:T(8,128)S(1)}, f32[2,4,8,128]{3,2,1,0:T(8,128)S(1)}) custom-call(f32[4096,128]{1,0:T(8,128)S(1)} %bitcast.16, f32[4,1024,128]{2,1,0:T(8,128)S(1)} %copy-done.14, bf16[1536,512]{1,0:T(8,128)(2,1)S(1)} %copy-done.17, f32[128,4,8,128]{3,2,1,0:T(8,128)S(1)} %copy-done.8, f32[128,4,8,128]{3,2,1,0:T(8,128)S(1)} %copy-done.10, ...), custom_call_target="tpu_custom_call" | custom-call | flops 1610612736 | bytes 12582912 | tf_op jit(solution)/shard_map/sweep/pallas_call | solution.py:350
  144.6 2.6 %collective-permute-start.3 = (f32[2,4,8,128]{3,2,1,0:T(8,128)S(1)}, f32[2,4,8,128]{3,2,1,0:T(8,128)S(1)}, u32[]{:S(2)}, u32[]{:S(2)}) collective-permute-start(f32[2,4,8,128]{3,2,1,0:T(8,128)S(1)} %get-tuple-element.19), channel_id=1, source_target_pairs={{0,2},{1,3},{2,0},{3,1},{4,6},{5,7},{6,4},{7,5},{8,10},{9,11},{10,... | collective-permute-start | bytes 98312 | tf_op jit(solution)/shard_map/ppermute | solution.py:360
  147.2 1.9 collective-permute-start.2
  149.1 11.4 %all-gather = f32[16,4,8,128]{3,2,1,0:T(8,128)S(1)} all-gather(f32[4,4,8,128]{3,2,1,0:T(8,128)S(1)} %get-tuple-element.20), channel_id=2, replica_groups=mesh['gx'=8,'gz'=8,'gy'=4] {'gy'}, dimensions={0}, use_global_device_ids=true | all-gather | bytes 327680 | tf_op jit(solution)/shard_map/all_gather | solution.py:338
  160.6 2.0 join.1
  162.6 56.6 %all_to_all.15 = f32[64,8,8,128]{3,2,1,0:T(8,128)S(1)} all-to-all(f32[64,8,8,128]{3,2,1,0:T(8,128)S(1)} %join.1), channel_id=1, replica_groups=mesh['gx'=8,'gz'=8,'gy'=4] {'gx','gz'}, dimensions={0} | all-to-all | bytes 4194304 | tf_op jit(solution)/shard_map/all_to_all | solution.py:270
  219.2 3.3 %flow_inverse.1 = f32[8,512,128]{2,1,0:T(8,128)} custom-call(f32[4096,128]{1,0:T(8,128)S(1)} %bitcast.17, bf16[512,1536]{1,0:T(8,128)(2,1)S(1)} %copy-done.16), custom_call_target="tpu_custom_call" | custom-call | flops 1610612736 | bytes 4194304 | tf_op jit(solution)/shard_map/flow_inverse/pallas_call | solution.py:384
  (40 shorter events, 7.0 us)
Async XLA Ops:
  0.0 2.8 %copy-start = (f32[3,8,512,128]{3,2,1,0:T(8,128)S(1)}, f32[3,8,512,128]{3,2,1,0:T(8,128)}, u32[]{:S(2)}) copy-start(f32[3,8,512,128]{3,2,1,0:T(8,128)} %w_ref.1) | copy-start | bytes 18874372
  2.8 1.4 copy-start.15
  7.7 63.4 %all-to-all-start.1 = ((f32[64,8,8,128]{3,2,1,0:T(8,128)}), f32[64,8,8,128]{3,2,1,0:T(8,128)}, u32[]{:S(2)}, u32[]{:S(2)}) async-start(f32[64,8,8,128]{3,2,1,0:T(8,128)} %span_field.1), calls=%async_computation.1 | async-start | bytes 4194304 | tf_op jit(solution)/shard_map/all_to_all | solution.py:270
  19.9 1.6 slice-start
  24.2 6.7 %collective-permute-start.1 = (f32[8,512]{1,0:T(8,128)S(1)}, f32[8,512]{1,0:T(8,128)S(1)}, u32[]{:S(2)}, u32[]{:S(2)}) collective-permute-start(f32[8,512]{1,0:T(8,128)S(1)} %get-tuple-element.21), channel_id=1, source_target_pairs={{1,0},{2,1},{3,2},{5,4},{6,5},{7,6},{9,8},{10,9},{11,10},{13,12},{... | collective-permute-start | bytes 49160 | tf_op jit(solution)/shard_map/ppermute | solution.py:293
  26.5 5.6 %collective-permute-start = (f32[8,512]{1,0:T(8,128)S(1)}, f32[8,512]{1,0:T(8,128)S(1)}, u32[]{:S(2)}, u32[]{:S(2)}) collective-permute-start(f32[8,512]{1,0:T(8,128)S(1)} %get-tuple-element.22), channel_id=1, source_target_pairs={{0,1},{1,2},{2,3},{4,5},{5,6},{6,7},{8,9},{9,10},{10,11},{12,13},{... | collective-permute-start | bytes 49160 | tf_op jit(solution)/shard_map/ppermute | solution.py:292
  32.1 2.8 %copy-start.1 = (f32[3,8,512,128]{3,2,1,0:T(8,128)S(1)}, f32[3,8,512,128]{3,2,1,0:T(8,128)}, u32[]{:S(2)}) copy-start(f32[3,8,512,128]{3,2,1,0:T(8,128)} %w_ref.1) | copy-start | bytes 18874372
  34.9 1.9 copy-start.2
  43.4 33.8 %copy-start.19 = (f32[4,128]{1,0:T(4,128)S(1)}, f32[4,128]{1,0:T(4,128)}, u32[]{:S(2)}) copy-start(f32[4,128]{1,0:T(4,128)} %constant.47) | copy-start | bytes 6148
  71.1 56.7 %all-to-all-start = ((f32[64,8,8,128]{3,2,1,0:T(8,128)}), f32[64,8,8,128]{3,2,1,0:T(8,128)S(1)}, u32[]{:S(2)}, u32[]{:S(2)}) async-start(f32[64,8,8,128]{3,2,1,0:T(8,128)} %flow_field.1), calls=%async_computation | async-start | bytes 4194304 | tf_op jit(solution)/shard_map/all_to_all | solution.py:270
  77.3 17.2 %copy-start.18 = (bf16[1536,512]{1,0:T(8,128)(2,1)S(1)}, bf16[1536,512]{1,0:T(8,128)(2,1)}, u32[]{:S(2)}) copy-start(bf16[1536,512]{1,0:T(8,128)(2,1)} %constant.43.clone.t_ref) | copy-start | bytes 4718596
  87.7 1.4 copy-start.3
  89.0 1.3 copy-start.5
  90.4 1.4 copy-start.7
  91.8 1.4 copy-start.9
  93.1 1.4 copy-start.11
  97.9 1.4 copy-start.13
  127.8 1.6 copy-start.8
  129.4 1.6 copy-start.10
  131.0 1.6 copy-start.12
  132.5 1.6 copy-start.14
  134.1 1.4 copy-start.17
  135.5 25.0 %copy-start.4 = (f32[4,1024,128]{2,1,0:T(8,128)S(1)}, f32[4,1024,128]{2,1,0:T(8,128)}, u32[]{:S(2)}) copy-start(f32[4,1024,128]{2,1,0:T(8,128)} %copy-done.3) | copy-start | bytes 6291460
  135.5 25.0 %copy-start.6 = (f32[4,1024,128]{2,1,0:T(8,128)S(1)}, f32[4,1024,128]{2,1,0:T(8,128)}, u32[]{:S(2)}) copy-start(f32[4,1024,128]{2,1,0:T(8,128)} %copy-done.5) | copy-start | bytes 6291460
  135.6 25.0 %copy-start.16 = (bf16[512,1536]{1,0:T(8,128)(2,1)S(1)}, bf16[512,1536]{1,0:T(8,128)(2,1)}, u32[]{:S(2)}) copy-start(bf16[512,1536]{1,0:T(8,128)(2,1)} %constant.45.clone.t_ref) | copy-start | bytes 4718596
  144.1 16.4 %collective-permute-start.4 = (f32[2,4,8,128]{3,2,1,0:T(8,128)S(1)}, f32[2,4,8,128]{3,2,1,0:T(8,128)S(1)}, u32[]{:S(2)}, u32[]{:S(2)}) collective-permute-start(f32[2,4,8,128]{3,2,1,0:T(8,128)S(1)} %get-tuple-element.19), channel_id=1, source_target_pairs={{0,3},{1,0},{2,1},{3,2},{4,7},{5,4},{6,5},{7,6},{8,11},{9,8},{10,9... | collective-permute-start | bytes 98312 | tf_op jit(solution)/shard_map/ppermute | solution.py:360
  144.6 15.9 %collective-permute-start.3 = (f32[2,4,8,128]{3,2,1,0:T(8,128)S(1)}, f32[2,4,8,128]{3,2,1,0:T(8,128)S(1)}, u32[]{:S(2)}, u32[]{:S(2)}) collective-permute-start(f32[2,4,8,128]{3,2,1,0:T(8,128)S(1)} %get-tuple-element.19), channel_id=1, source_target_pairs={{0,2},{1,3},{2,0},{3,1},{4,6},{5,7},{6,4},{7,5},{8,10},{9,11},{10,... | collective-permute-start | bytes 98312 | tf_op jit(solution)/shard_map/ppermute | solution.py:360
  147.2 13.3 %collective-permute-start.2 = (f32[2,4,8,128]{3,2,1,0:T(8,128)S(1)}, f32[2,4,8,128]{3,2,1,0:T(8,128)S(1)}, u32[]{:S(2)}, u32[]{:S(2)}) collective-permute-start(f32[2,4,8,128]{3,2,1,0:T(8,128)S(1)} %get-tuple-element.19), channel_id=1, source_target_pairs={{0,1},{1,2},{2,3},{3,0},{4,5},{5,6},{6,7},{7,4},{8,9},{9,10},{10,1... | collective-permute-start | bytes 98312 | tf_op jit(solution)/shard_map/ppermute | solution.py:360
where the time goes:
time: 224 us; the launch traced here: 222 us
  blocking collectives  68 us (30%)
  waiting for transfers between devices  57.4 us (26%)
  Pallas kernels  37.7 us (17%)
  local copies, waits for them, and re-layouts  30.6 us (14%)
  starting transfers between devices  28.4 us (13%)
    all_to_all x1, blocking collectives, moved(): return lax.all_to_all(x, both, split_axis=0, concat_axis=0, tiled=True)  56.6 us
    all_to_all x2, waiting for transfers between devices, moved(): return lax.all_to_all(x, both, split_axis=0, concat_axis=0, tiled=True)  56.2 us
    unnamed x41, local copies, waits for them, and re-layouts  26.8 us
    all_to_all x2, starting transfers between devices, moved(): return lax.all_to_all(x, both, split_axis=0, concat_axis=0, tiled=True)  17.5 us
    all_gather x1, blocking collectives, local(): vw = lax.all_gather(vw_ends, 'gy', axis=0, tiled=False)  11.4 us
    pallas_call x1, Pallas kernels, local(): pl.pallas_call(factor_kernel, in_specs=[smem, smem, vmem], out_specs=[vme...  10.4 us
    pallas_call x1, Pallas kernels, local(): pl.pallas_call(sweep_kernel, in_specs=[vmem] * 6, out_specs=[vmem] * 2, o...  8.54 us
    pallas_call x1, Pallas kernels, local(): pl.pallas_call(flow_field_kernel, grid=(planes // 2,), in_specs=[plane_bl...  6.56 us
  transfers between devices with their start and end apart: 7, of which 3 were waited for; matrix products, arithmetic and copies ran while one was open for 2% of the time, Pallas kernels for 9%

commit v1 on v0

--- a/solution.py
+++ b/solution.py
@@ -137,72 +137,154 @@
         ends_ref[3, t] = w_ref[t, pl.ds(rows - 1, 8, stride=rows), :]
 
 
-def span_modes(x_ref, t_ref, mode):
+def span_modes(x_ref, table, mode):
     planes = x_ref.shape[0] // 8
     both = [
         jnp.transpose(x_ref[pl.ds(mode + p, planes, stride=8), :]) for p in range(2)
     ]
     x = jnp.concatenate(both, axis=0)
-    return jnp.dot(parts(x, 1), t_ref[...], preferred_element_type=f32)
+    return jnp.dot(parts(x, 1), table, preferred_element_type=f32)
 
 
 def span_first_kernel(x_ref, t_ref, o_ref):
     tiles = o_ref.shape[0]
     for mode in range(0, 8, 2):
-        y = span_modes(x_ref, t_ref, mode)
+        y = span_modes(x_ref, t_ref[...], mode)
         for t in range(tiles):
             o_ref[t, mode * 128 : (mode + 2) * 128, :] = y[:, t * 128 : (t + 1) * 128]
 
 
-def sweep_kernel(x_ref, s_ref, t_ref, inv_ref, m_ref, r_ref, o_ref, ends_ref):
+def pair_copies(hbm, held, sems, first):
+    out = []
+    for pair in range(4):
+        part = pl.ds(pair * 256, 256)
+        out.append(
+            pltpu.make_async_copy(hbm.at[:, part, :], held.at[:, part, :], sems.at[first + pair])
+        )
+    return out
+
+
+def source_kernel(
+    x_ref, weight_ref, gap_ref, t_hbm, s_hbm, v_hbm, w_hbm, o_ref, ends_ref, t, s, v, w, sems
+):
     tiles = o_ref.shape[0]
-    rows = inv_ref.shape[0]
-    for mode in range(0, 8, 2):
-        y = span_modes(x_ref, t_ref, mode)
-        part = slice(mode * 128, (mode + 2) * 128)
-        for t in range(tiles):
-            o_ref[t, part, :] = y[:, t * 128 : (t + 1) * 128] + s_ref[t, part, :]
-
-    def ahead(y, carry):
-        out = []
-        for t in range(tiles):
-            side = o_ref[t, pl.ds(y, 8, stride=rows), :]
-            val = side * inv_ref[y, t] - m_ref[y, t] * carry[t]
-            o_ref[t, pl.ds(y, 8, stride=rows), :] = val
-            out.append(val)
-        return tuple(out)
-
-    zero = jnp.zeros((8, 128), f32)
-    lax.fori_loop(0, rows, ahead, (zero,) * tiles, unroll=4)
-
-    def back(s, carry):
-        y = rows - 1 - s
-        out = []
-        for t in range(tiles):
-            val = o_ref[t, pl.ds(y, 8, stride=rows), :] - r_ref[y, t] * carry[t]
-            o_ref[t, pl.ds(y, 8, stride=rows), :] = val
-            out.append(val)
-        return tuple(out)
-
-    first = lax.fori_loop(0, rows, back, (zero,) * tiles, unroll=4)
-    for t in range(tiles):
-        ends_ref[0, t] = first[t]
-        ends_ref[1, t] = o_ref[t, pl.ds(rows - 1, 8, stride=rows), :]
-
-
-def join_kernel(me_ref, y_ref, v_ref, w_ref, ys_ref, vw_ref, t_ref, o_ref, b_ref, f_ref):
+    table = pltpu.make_async_copy(t_hbm, t, sems.at[0])
+    table.start()
+    copies = list(
+        zip(
+            pair_copies(s_hbm, s, sems, 1),
+            pair_copies(v_hbm, v, sems, 5),
+            pair_copies(w_hbm, w, sems, 9),
+        )
+    )
+    for group in copies:
+        for copy in group:
+            copy.start()
+    table.wait()
+    weight = weight_ref[...]
+    for pair in range(4):
+        y = span_modes(x_ref, t[...], 2 * pair)
+        for copy in copies[pair]:
+            copy.wait()
+        for p in range(2):
+            mode = 2 * pair + p
+            part = slice(mode * 128, (mode + 1) * 128)
+            for tile in range(tiles):
+                side = y[p * 128 : (p + 1) * 128, tile * 128 : (tile + 1) * 128] + s[tile, part, :]
+                o_ref[tile, part, :] = side
+                side = side * weight
+                row = slice(mode, mode + 1)
+                ends_ref[0, tile, row, :] = -gap_ref[0] * jnp.sum(
+                    side * v[tile, part, :], axis=0, keepdims=True
+                )
+                ends_ref[1, tile, row, :] = -gap_ref[1] * jnp.sum(
+                    side * w[tile, part, :], axis=0, keepdims=True
+                )
+
+
+def sweep_kernel(x_ref, inv_hbm, m_hbm, r_hbm, o_ref, inv, m, r, held, sems):
+    tiles = o_ref.shape[0]
+    rows = inv.shape[0]
+    count = 4
+    chunk = rows // count
+
+    def copies(hbm, here, first):
+        return [
+            pltpu.make_async_copy(
+                hbm.at[pl.ds(c * chunk, chunk)], here.at[pl.ds(c * chunk, chunk)], sems.at[first + c]
+            )
+            for c in range(count)
+        ]
+
+    invs, ms, rs = copies(inv_hbm, inv, 0), copies(m_hbm, m, count), copies(r_hbm, r, 2 * count)
+    for c in range(count):
+        invs[c].start()
+        ms[c].start()
+    for c in range(count - 1, -1, -1):
+        rs[c].start()
+
+    def ahead(block, carry):
+        for j in range(8):
+            y = block * 8 + j
+            out = []
+            for t in range(tiles):
+                side = x_ref[t, pl.ds(y, 8, stride=rows), :]
+                val = side * inv[y, t] - m[y, t] * carry[t]
+                held[y, t] = val
+                out.append(val)
+            carry = tuple(out)
+        return carry
+
+    carry = (jnp.zeros((8, 128), f32),) * tiles
+    for c in range(count):
+        invs[c].wait()
+        ms[c].wait()
+        carry = lax.fori_loop(c * chunk // 8, (c + 1) * chunk // 8, ahead, carry)
+
+    def back(step, carry):
+        for j in range(8):
+            y = rows - 1 - (step * 8 + j)
+            out = []
+            for t in range(tiles):
+                val = held[y, t] - r[y, t] * carry[t]
+                o_ref[t, pl.ds(y, 8, stride=rows), :] = val
+                out.append(val)
+            carry = tuple(out)
+        return carry
+
+    carry = (jnp.zeros((8, 128), f32),) * tiles
+    for c in range(count):
+        rs[count - 1 - c].wait()
+        carry = lax.fori_loop(c * chunk // 8, (c + 1) * chunk // 8, back, carry)
+
+
+def join_kernel(me_ref, y_ref, *refs):
+    ends, (vw_ref, v_hbm, w_hbm, t_hbm, o_ref, ys_ref, b_ref, f_ref, v, w, t, sems) = (
+        refs[:-12],
+        refs[-12:],
+    )
     blocks = vw_ref.shape[0]
     tiles = y_ref.shape[0]
     me = me_ref[0]
-    for t in range(tiles):
+    table = pltpu.make_async_copy(t_hbm, t, sems.at[0])
+    copies = list(zip(pair_copies(v_hbm, v, sems, 1), pair_copies(w_hbm, w, sems, 5)))
+    for copy in copies[0]:
+        copy.start()
+    table.start()
+    for group in copies[1:]:
+        for copy in group:
+            copy.start()
+    for shift in range(blocks):
+        ys_ref[shift] = ends[shift][...]
+    for tile in range(tiles):
         alpha = jnp.zeros((8, 128), f32)
         beta = jnp.zeros((8, 128), f32)
         alphas, betas, starts, scales = [], [], [], []
         for g in range(blocks):
             slot = lax.rem(me + blocks - g, blocks)
-            yf = ys_ref[slot, 0, t]
-            yb = ys_ref[slot, 1, t]
-            vf, vb, wf, wb = (vw_ref[g, n, t] for n in range(4))
+            yf = ys_ref[slot, 0, tile]
+            yb = ys_ref[slot, 1, tile]
+            vf, vb, wf, wb = (vw_ref[slot, n, tile] for n in range(4))
             scale = 1.0 / (1.0 - vf * beta)
             start = (yf + vf * alpha) * scale
             starts.append(start)
@@ -214,40 +296,45 @@
             alphas.append(alpha)
             betas.append(beta)
         after = jnp.zeros((8, 128), f32)
-        f_ref[blocks, t] = after
-        b_ref[0, t] = after
+        f_ref[blocks, tile] = after
+        b_ref[0, tile] = after
         for g in range(blocks - 1, -1, -1):
-            b_ref[g + 1, t] = alphas[g] + betas[g] * after
+            b_ref[g + 1, tile] = alphas[g] + betas[g] * after
             after = starts[g] + scales[g] * after
-            f_ref[g, t] = after
-    for mode in range(0, 8, 2):
+            f_ref[g, tile] = after
+    for pair in range(4):
+        for copy in copies[pair]:
+            copy.wait()
+        if pair == 0:
+            table.wait()
         columns = []
-        for t in range(tiles):
+        for tile in range(tiles):
             both = []
             for p in range(2):
-                part = slice((mode + p) * 128, (mode + p + 1) * 128)
-                left = b_ref[me, t, pl.ds(mode + p, 1), :]
-                right = f_ref[me + 1, t, pl.ds(mode + p, 1), :]
-                both.append(y_ref[t, part, :] + v_ref[t, part, :] * left + w_ref[t, part, :] * right)
+                mode = 2 * pair + p
+                part = slice(mode * 128, (mode + 1) * 128)
+                left = b_ref[me, tile, pl.ds(mode, 1), :]
+                right = f_ref[me + 1, tile, pl.ds(mode, 1), :]
+                both.append(
+                    y_ref[tile, part, :] + v[tile, part, :] * left + w[tile, part, :] * right
+                )
             columns.append(jnp.concatenate(both, axis=0))
         x = jnp.concatenate(columns, axis=1)
         y = lax.dot_general(
-            t_ref[...], parts(x, 1), (((1,), (1,)), ((), ())), preferred_element_type=f32
+            t[...], parts(x, 1), (((1,), (1,)), ((), ())), preferred_element_type=f32
         )
         for p in range(2):
             part = y[:, 128 * p : 128 * (p + 1)]
-            o_ref[:, mode + p] = part.reshape(part.shape[0] // 8, 8, 128)
+            o_ref[:, 2 * pair + p] = part.reshape(part.shape[0] // 8, 8, 128)
 
 
 def flow_inverse_kernel(x_ref, t_ref, o_ref):
     slots = x_ref.shape[0] // 8
-    for plane in range(0, 8, 2):
-        x = jnp.concatenate(
-            [x_ref[pl.ds(plane + p, slots, stride=8), :] for p in range(2)], axis=1
-        )
-        y = jnp.dot(t_ref[...], parts(x, 0), preferred_element_type=f32)
-        for p in range(2):
-            o_ref[plane + p] = y[:, 128 * p : 128 * (p + 1)]
+    plane = pl.program_id(0) * 2
+    x = jnp.concatenate([x_ref[pl.ds(plane + p, slots, stride=8), :] for p in range(2)], axis=1)
+    y = jnp.dot(t_ref[...], parts(x, 0), preferred_element_type=f32)
+    for p in range(2):
+        o_ref[p] = y[:, 128 * p : 128 * (p + 1)]
 
 
 def local(velocity, spacing):
@@ -280,7 +367,7 @@
         in_specs=[plane_block(2), whole(*table.shape)],
         out_specs=out_block,
         out_shape=field_shape,
-        compiler_params=params(32),
+        compiler_params=params(58),
         cost_estimate=cost(field_flops, 2 * field_bytes),
         name="span_field",
     )(velocity, table)
@@ -311,7 +398,7 @@
         ],
         out_specs=out_block,
         out_shape=field_shape,
-        compiler_params=params(40),
+        compiler_params=params(58),
         cost_estimate=cost(2 * field_flops, 3 * field_bytes),
         name="flow_field",
     )(velocity, velocity, before, after, width.reshape(1, rows), flow_table)
@@ -331,65 +418,103 @@
         out_shape=[step_shape] * 3
         + [slab_shape] * 2
         + [jax.ShapeDtypeStruct((4, tiles, modes, 128), f32)],
-        compiler_params=params(32),
+        compiler_params=params(58),
         cost_estimate=cost(field_flops, 5 * field_bytes),
         name="factor",
     )(lower, upper, sigma)
-    vw = lax.all_gather(vw_ends, "gy", axis=0, tiled=False)
+    rings = [[(i, (i + n) % blocks) for i in range(blocks)] for n in range(1, blocks)]
+    vw = jnp.stack([vw_ends] + [lax.ppermute(vw_ends, "gy", ring) for ring in rings])
+    span_here, vw = lax.optimization_barrier((span_here, vw))
 
     flat = (span_length * modes, rows)
+    hbm = pl.BlockSpec(memory_space=pltpu.HBM)
     span_source = pl.pallas_call(
         span_first_kernel,
         in_specs=[vmem, vmem],
         out_specs=vmem,
         out_shape=slab_shape,
-        compiler_params=params(32),
+        compiler_params=params(58),
         cost_estimate=cost(field_flops, 2 * field_bytes),
         name="span_first",
     )(span_here.reshape(flat), jnp.asarray(right_table(span_derive)))
-    y_all, y_ends = pl.pallas_call(
-        sweep_kernel,
-        in_specs=[vmem] * 6,
+    slab = pltpu.VMEM(slab_shape.shape, f32)
+    weight = jnp.broadcast_to((0.5 * width)[:, None], (rows, 128))
+    end_gaps = jnp.stack([gaps[0], gaps[rows]])
+    source, y_ends = pl.pallas_call(
+        source_kernel,
+        in_specs=[vmem, vmem, smem] + [hbm] * 4,
         out_specs=[vmem] * 2,
         out_shape=[slab_shape, jax.ShapeDtypeStruct((2, tiles, modes, 128), f32)],
-        compiler_params=params(40),
-        cost_estimate=cost(field_flops, 6 * field_bytes),
+        scratch_shapes=[
+            pltpu.VMEM((3 * span_length, span_length), bf16),
+            slab,
+            slab,
+            slab,
+            pltpu.SemaphoreType.DMA((13,)),
+        ],
+        compiler_params=params(32),
+        cost_estimate=cost(field_flops, 5 * field_bytes),
+        name="source",
+    )(
+        flow_here.reshape(flat),
+        weight,
+        end_gaps,
+        jnp.asarray(right_table(span_forward)),
+        span_source,
+        v_all,
+        w_all,
+    )
+    ends = [y_ends] + [lax.ppermute(y_ends, "gy", ring) for ring in rings]
+    step = pltpu.VMEM(step_shape.shape, f32)
+    y_all = pl.pallas_call(
+        sweep_kernel,
+        in_specs=[vmem] + [hbm] * 3,
+        out_specs=vmem,
+        out_shape=slab_shape,
+        scratch_shapes=[step] * 4 + [pltpu.SemaphoreType.DMA((12,))],
+        compiler_params=params(32),
+        cost_estimate=cost(field_flops, 5 * field_bytes),
         name="sweep",
-    )(flow_here.reshape(flat), span_source, jnp.asarray(right_table(span_forward)), inv, m, r)
-    shifted = [y_ends] + [
-        lax.ppermute(y_ends, "gy", [(i, (i + s) % blocks) for i in range(blocks)])
-        for s in range(1, blocks)
-    ]
-    ys = jnp.stack(shifted)
+    )(source, inv, m, r)
     end_shape = (blocks + 1, tiles, modes, 128)
     back_sent = pl.pallas_call(
         join_kernel,
-        in_specs=[smem] + [vmem] * 6,
+        in_specs=[smem] + [vmem] * (2 + blocks) + [hbm] * 3,
         out_specs=vmem,
         out_shape=jax.ShapeDtypeStruct((group, modes, planes, rows), f32),
-        scratch_shapes=[pltpu.VMEM(end_shape, f32), pltpu.VMEM(end_shape, f32)],
-        compiler_params=params(40),
+        scratch_shapes=[
+            pltpu.VMEM((blocks, 2, tiles, modes, 128), f32),
+            pltpu.VMEM(end_shape, f32),
+            pltpu.VMEM(end_shape, f32),
+            slab,
+            slab,
+            pltpu.VMEM((span_length, 3 * span_length), bf16),
+            pltpu.SemaphoreType.DMA((9,)),
+        ],
+        compiler_params=params(32),
         cost_estimate=cost(field_flops, 4 * field_bytes),
         name="join",
     )(
         me.reshape(1).astype(jnp.int32),
         y_all,
+        *ends,
+        vw,
         v_all,
         w_all,
-        ys,
-        vw,
         jnp.asarray(left_table(span_inverse.T)),
     )
     back_here = moved(back_sent)
+    last_table = jnp.asarray(left_table(flow_inverse.T))
     return pl.pallas_call(
         flow_inverse_kernel,
-        in_specs=[vmem, vmem],
-        out_specs=vmem,
+        grid=(planes // 2,),
+        in_specs=[whole(flow_length * planes, rows), whole(*last_table.shape)],
+        out_specs=pl.BlockSpec((2, flow_length, rows), lambda i: (i, 0, 0)),
         out_shape=jax.ShapeDtypeStruct((planes, flow_length, rows), f32),
         compiler_params=params(32),
         cost_estimate=cost(field_flops, 2 * field_bytes),
         name="flow_inverse",
-    )(back_here.reshape(flow_length * planes, rows), jnp.asarray(left_table(flow_inverse.T)))
+    )(back_here.reshape(flow_length * planes, rows), last_table)
 
 
 def solution(mesh):

time: 224 us -> 211 us (0.942)
  local copies, waits for them, and re-layouts: 30.6 us -> 13.3 us
  Pallas kernels: 37.7 us -> 50.5 us
  blocking collectives: 68 us -> 56.5 us
  waiting for transfers between devices: 57.4 us -> 52.1 us
  starting transfers between devices: 28.4 us -> 33.3 us
  other arithmetic: 0.16 us -> 4.07 us
    unnamed x41 -> x29, local copies, waits for them, and re-layouts: 26.8 us -> 8.77 us
    all_gather x1 -> x0, blocking collectives: 11.4 us -> none  [local(): vw = lax.all_gather(vw_ends, 'gy', axis=0, tiled=False)]
    all_to_all x2, waiting for transfers between devices: 56.2 us -> 50.8 us  [moved(): return lax.all_to_all(x, both, split_axis=0, concat_axis=0, tiled=True)]
    ppermute x3 -> x6, starting transfers between devices: 5 us -> 9.93 us  [the longest x3 5 us: local(): ends = [y_ends] + [lax.ppermute(y_ends, 'gy', ring) for ring in rings]]
    pallas_call x1, Pallas kernels: 10.4 us -> 14.5 us  [local(): pl.pallas_call(factor_kernel, in_specs=[smem, smem, vmem], out_specs=[vme...]
    pallas_call x3 -> x4, Pallas kernels: 13.8 us -> 16.4 us  [the longest x1 4.57 us: local(): pl.pallas_call(join_kernel, in_specs=[smem] + [vmem] * (2 + blocks) + [hb...]
    pallas_call x1, Pallas kernels: 6.56 us -> 8.87 us  [local(): pl.pallas_call(flow_field_kernel, grid=(planes // 2,), in_specs=[plane_bl...]
  transfers between devices with their start and end apart: 7 -> 10, of which waited for: 3 -> 4; matrix products, arithmetic and copies ran while one was open for 2% -> 4% of each run, Pallas kernels for 9% -> 16%
where the time goes in v1:
time: 211 us; the launch traced here: 210 us
  blocking collectives  56.5 us (27%)
  waiting for transfers between devices  52.1 us (25%)
  Pallas kernels  50.5 us (24%)
  starting transfers between devices  33.3 us (16%)
  local copies, waits for them, and re-layouts  13.3 us (6%)
  other arithmetic  4.07 us (2%)
    all_to_all x1, blocking collectives, moved(): return lax.all_to_all(x, both, split_axis=0, concat_axis=0, tiled=True)  56.5 us
    all_to_all x2, waiting for transfers between devices, moved(): return lax.all_to_all(x, both, split_axis=0, concat_axis=0, tiled=True)  50.8 us
    all_to_all x2, starting transfers between devices, moved(): return lax.all_to_all(x, both, split_axis=0, concat_axis=0, tiled=True)  17.5 us
    pallas_call x1, Pallas kernels, local(): pl.pallas_call(factor_kernel, in_specs=[smem, smem, vmem], out_specs=[vme...  14.5 us
    pallas_call x1, Pallas kernels, local(): pl.pallas_call(flow_field_kernel, grid=(planes // 2,), in_specs=[plane_bl...  8.87 us
    unnamed x29, local copies, waits for them, and re-layouts  8.77 us
    pallas_call x1, Pallas kernels, local(): pl.pallas_call(span_field_kernel, grid=(planes // 2,), in_specs=[plane_bl...  5.49 us
    pallas_call x1, Pallas kernels, local(): pl.pallas_call(span_first_kernel, in_specs=[vmem, vmem], out_specs=vmem,...  5.2 us
  transfers between devices with their start and end apart: 10, of which 4 were waited for; matrix products, arithmetic and copies ran while one was open for 4% of the time, Pallas kernels for 16%

profile of v1, /device:TPU:8, one launch (start us, length us, event | category | flops | bytes accessed | tf_op | source)
XLA Modules:
  0.0 209.9 jit_solution(11139132312211605926)
XLA Ops:
  0.0 5.5 %span_field.1 = f32[64,8,8,128]{3,2,1,0:T(8,128)} custom-call(f32[3,8,512,128]{3,2,1,0:T(8,128)} %w_ref.1, bf16[512,1536]{1,0:T(8,128)(2,1)} %constant.41.clone.t_ref), custom_call_target="tpu_custom_call" | custom-call | flops 1610612736 | bytes 4194304 | tf_op jit(solution)/shard_map/span_field/pallas_call | solution.py:364
  5.5 12.2 %all-to-all-start.1 = ((f32[64,8,8,128]{3,2,1,0:T(8,128)}), f32[64,8,8,128]{3,2,1,0:T(8,128)}, u32[]{:S(2)}, u32[]{:S(2)}) async-start(f32[64,8,8,128]{3,2,1,0:T(8,128)} %span_field.1), calls=%async_computation.1 | async-start | bytes 4194304 | tf_op jit(solution)/shard_map/all_to_all | solution.py:357
  17.7 1.6 slice-done
  19.3 2.0 copy.12
  21.2 0.7 slice_bitcast_fusion
  22.0 2.3 %collective-permute-start.1 = (f32[8,512]{1,0:T(8,128)S(1)}, f32[8,512]{1,0:T(8,128)S(1)}, u32[]{:S(2)}, u32[]{:S(2)}) collective-permute-start(f32[8,512]{1,0:T(8,128)S(1)} %get-tuple-element.27), channel_id=1, source_target_pairs={{1,0},{2,1},{3,2},{5,4},{6,5},{7,6},{9,8},{10,9},{11,10},{13,12},{... | collective-permute-start | bytes 49160 | tf_op jit(solution)/shard_map/ppermute | solution.py:380
  24.3 3.5 %collective-permute-start = (f32[8,512]{1,0:T(8,128)S(1)}, f32[8,512]{1,0:T(8,128)S(1)}, u32[]{:S(2)}, u32[]{:S(2)}) collective-permute-start(f32[8,512]{1,0:T(8,128)S(1)} %get-tuple-element.28), channel_id=1, source_target_pairs={{0,1},{1,2},{2,3},{4,5},{5,6},{6,7},{8,9},{9,10},{10,11},{12,13},{... | collective-permute-start | bytes 49160 | tf_op jit(solution)/shard_map/ppermute | solution.py:379
  27.8 0.8 dynamic_slice.6
  29.3 0.7 collective-permute-done.before_ref
  30.6 8.9 %flow_field.1 = f32[64,8,8,128]{3,2,1,0:T(8,128)} custom-call(f32[3,8,512,128]{3,2,1,0:T(8,128)} %w_ref.1, f32[3,8,512,128]{3,2,1,0:T(8,128)} %w_ref.1, f32[8,512]{1,0:T(8,128)} %copy-done.11, f32[8,512]{1,0:T(8,128)} %copy-done.10, f32[1,128]{1,0:T(1,128)} %bitcast.21, bf16[512,3072]{1,0:T(8,128)(2,1)} %constant.42.clone.t_ref), custom_call_target="tpu_custom_call" | custom-call | flops 3221225472 | bytes 6291456 | tf_op jit(solution)/shard_map/flow_field/pallas_call | solution.py:388
  39.5 29.4 %all-to-all-done.1 = f32[64,8,8,128]{3,2,1,0:T(8,128)} async-done(((f32[64,8,8,128]{3,2,1,0:T(8,128)}), f32[64,8,8,128]{3,2,1,0:T(8,128)}, u32[]{:S(2)}, u32[]{:S(2)}) %all-to-all-start.1) | async-done | bytes 2097184 | tf_op jit(solution)/shard_map/all_to_all | solution.py:357
  68.9 5.3 %all-to-all-start = ((f32[64,8,8,128]{3,2,1,0:T(8,128)}), f32[64,8,8,128]{3,2,1,0:T(8,128)S(1)}, u32[]{:S(2)}, u32[]{:S(2)}) async-start(f32[64,8,8,128]{3,2,1,0:T(8,128)} %flow_field.1), calls=%async_computation | async-start | bytes 4194304 | tf_op jit(solution)/shard_map/all_to_all | solution.py:357
  74.2 0.8 dynamic_slice.7
  75.5 0.7 broadcast_add_fusion.sigma_ref
  76.2 14.5 %factor.1 = (f32[128,4,8,128]{3,2,1,0:T(8,128)}, f32[128,4,8,128]{3,2,1,0:T(8,128)}, f32[128,4,8,128]{3,2,1,0:T(8,128)}, f32[4,1024,128]{2,1,0:T(8,128)}, f32[4,...) custom-call(f32[128]{0:T(128)} %get-tuple-element.31.low_ref, f32[128]{0:T(128)} %get-tuple-element.25.up_ref, ...), custom_call_target="tpu_custom_call" | custom-call | flops 1610612736 | bytes 10485760 | tf_op jit(solution)/shard_map/factor/pallas_call | solution.py:414
  91.2 2.6 %collective-permute-start.3 = (f32[4,4,8,128]{3,2,1,0:T(8,128)}, f32[4,4,8,128]{3,2,1,0:T(8,128)S(1)}, u32[]{:S(2)}, u32[]{:S(2)}) collective-permute-start(f32[4,4,8,128]{3,2,1,0:T(8,128)} %get-tuple-element.15), channel_id=1, source_target_pairs={{0,2},{1,3},{2,0},{3,1},{4,6},{5,7},{6,4},{7,5},{8,10},{9,11},{10,... | collective-permute-start | bytes 196616 | tf_op jit(solution)/shard_map/ppermute | solution.py:426
  93.8 1.9 collective-permute-start.2
  96.2 1.4 pad_maximum_fusion.1.gap_ref
  98.2 0.9 pad_maximum_fusion.refs_4_
  99.1 5.2 %span_first.1.s_hbm = f32[4,1024,128]{2,1,0:T(8,128)} custom-call(f32[4096,128]{1,0:T(8,128)} %bitcast.10.x_ref, bf16[1536,512]{1,0:T(8,128)(2,1)} %constant.45.clone.t_ref), custom_call_target="tpu_custom_call" | custom-call | flops 1610612736 | bytes 4194304 | tf_op jit(solution)/shard_map/span_first/pallas_call | solution.py:431
  104.3 21.3 %all-to-all-done = f32[64,8,8,128]{3,2,1,0:T(8,128)S(1)} async-done(((f32[64,8,8,128]{3,2,1,0:T(8,128)}), f32[64,8,8,128]{3,2,1,0:T(8,128)S(1)}, u32[]{:S(2)}, u32[]{:S(2)}) %all-to-all-start) | async-done | bytes 2097184 | tf_op jit(solution)/shard_map/all_to_all | solution.py:357
  125.7 1.6 copy-done
  127.3 1.6 copy-done.2
  128.9 1.6 copy-done.7
  130.5 1.4 copy-done.8
  131.9 4.2 %source.1 = (f32[4,1024,128]{2,1,0:T(8,128)S(1)}, f32[2,4,8,128]{3,2,1,0:T(8,128)S(1)}) custom-call(f32[4096,128]{1,0:T(8,128)S(1)} %bitcast.14, f32[128,128]{1,0:T(8,128)S(1)} %broadcast_in_dim.2.weight_ref, f32[2]{0:T(128)S(1)} %pad_maximum_fusion.1.gap_ref, bf16[1536,512]{1,0:T(8,128)(2,1)S(1)} %copy-done.8, f32[4,1024,128]{2,1,0:T(8,128)S(1)} %copy-done.7, ...), custom_call_target="tpu_custom_call" | custom-call | flops 1610612736 | bytes 10485760 | tf_op jit(solution)/shard_map/source/pallas_call | solution.py:443
  136.6 2.6 %collective-permute-start.6 = (f32[2,4,8,128]{3,2,1,0:T(8,128)S(1)}, f32[2,4,8,128]{3,2,1,0:T(8,128)S(1)}, u32[]{:S(2)}, u32[]{:S(2)}) collective-permute-start(f32[2,4,8,128]{3,2,1,0:T(8,128)S(1)} %get-tuple-element.23.refs_0_), channel_id=1, source_target_pairs={{0,2},{1,3},{2,0},{3,1},{4,6},{5,7},{6,4},{7,5},{8,10},{9,11},{10,... | collective-permute-start | bytes 98312 | tf_op jit(solution)/shard_map/ppermute | solution.py:467
  139.2 1.9 collective-permute-start.5
  141.1 4.1 %sweep.1.y_ref = f32[4,1024,128]{2,1,0:T(8,128)S(1)} custom-call(f32[4,1024,128]{2,1,0:T(8,128)S(1)} %get-tuple-element.19.x_ref, f32[128,4,8,128]{3,2,1,0:T(8,128)S(1)} %copy-done.4, f32[128,4,8,128]{3,2,1,0:T(8,128)S(1)} %copy-done.5, f32[128,4,8,128]{3,2,1,0:T(8,128)S(1)} %copy-done.6), custom_call_target="tpu_custom_call" | custom-call | flops 1610612736 | bytes 10485760 | tf_op jit(solution)/shard_map/sweep/pallas_call | solution.py:469
  145.3 4.6 %join.1 = f32[64,8,8,128]{3,2,1,0:T(8,128)S(1)} custom-call(s32[1]{0:T(128)} %bitcast.me_ref, f32[4,1024,128]{2,1,0:T(8,128)S(1)} %sweep.1.y_ref, f32[2,4,8,128]{3,2,1,0:T(8,128)S(1)} %get-tuple-element.23.refs_0_, f32[2,4,8,128]{3,2,1,0:T(8,128)S(1)} %collective-permute-done.5.refs_1_, f32[2,4,8,128]{3,2,1,0:T(8,128)S(1)} %collective-permute-done.6.refs_2_, ...), custom_call_target="tpu_custom_call" | custom-call | flops 1610612736 | bytes 8388608 | tf_op jit(solution)/shard_map/join/pallas_call | solution.py:480
  149.9 56.5 %all_to_all.15 = f32[64,8,8,128]{3,2,1,0:T(8,128)S(1)} all-to-all(f32[64,8,8,128]{3,2,1,0:T(8,128)S(1)} %join.1), channel_id=1, replica_groups=mesh['gx'=8,'gz'=8,'gy'=4] {'gx','gz'}, dimensions={0} | all-to-all | bytes 4194304 | tf_op jit(solution)/shard_map/all_to_all | solution.py:357
  206.4 3.5 %flow_inverse.1 = f32[8,512,128]{2,1,0:T(8,128)} custom-call(f32[4096,128]{1,0:T(8,128)S(1)} %bitcast.15, bf16[512,1536]{1,0:T(8,128)(2,1)S(1)} %copy-done.9), custom_call_target="tpu_custom_call" | custom-call | flops 1610612736 | bytes 4194304 | tf_op jit(solution)/shard_map/flow_inverse/pallas_call | solution.py:508
  (38 shorter events, 4.1 us)
Async XLA Ops:
  5.5 63.4 %all-to-all-start.1 = ((f32[64,8,8,128]{3,2,1,0:T(8,128)}), f32[64,8,8,128]{3,2,1,0:T(8,128)}, u32[]{:S(2)}, u32[]{:S(2)}) async-start(f32[64,8,8,128]{3,2,1,0:T(8,128)} %span_field.1), calls=%async_computation.1 | async-start | bytes 4194304 | tf_op jit(solution)/shard_map/all_to_all | solution.py:357
  17.7 1.6 slice-start
  22.0 7.3 %collective-permute-start.1 = (f32[8,512]{1,0:T(8,128)S(1)}, f32[8,512]{1,0:T(8,128)S(1)}, u32[]{:S(2)}, u32[]{:S(2)}) collective-permute-start(f32[8,512]{1,0:T(8,128)S(1)} %get-tuple-element.27), channel_id=1, source_target_pairs={{1,0},{2,1},{3,2},{5,4},{6,5},{7,6},{9,8},{10,9},{11,10},{13,12},{... | collective-permute-start | bytes 49160 | tf_op jit(solution)/shard_map/ppermute | solution.py:380
  24.3 5.6 %collective-permute-start = (f32[8,512]{1,0:T(8,128)S(1)}, f32[8,512]{1,0:T(8,128)S(1)}, u32[]{:S(2)}, u32[]{:S(2)}) collective-permute-start(f32[8,512]{1,0:T(8,128)S(1)} %get-tuple-element.28), channel_id=1, source_target_pairs={{0,1},{1,2},{2,3},{4,5},{5,6},{6,7},{8,9},{9,10},{10,11},{12,13},{... | collective-permute-start | bytes 49160 | tf_op jit(solution)/shard_map/ppermute | solution.py:379
  29.3 0.7 copy-start.10
  30.0 0.6 copy-start.11
  39.4 35.6 %copy-start.12 = (f32[128]{0:T(128)S(1)}, f32[128]{0:T(128)}, u32[]{:S(2)}) copy-start(f32[128]{0:T(128)} %get-tuple-element.26) | copy-start | bytes 1540
  39.4 36.1 %copy-start.13 = (f32[4,128]{1,0:T(4,128)S(1)}, f32[4,128]{1,0:T(4,128)}, u32[]{:S(2)}) copy-start(f32[4,128]{1,0:T(4,128)} %constant.49) | copy-start | bytes 6148
  68.9 56.7 %all-to-all-start = ((f32[64,8,8,128]{3,2,1,0:T(8,128)}), f32[64,8,8,128]{3,2,1,0:T(8,128)S(1)}, u32[]{:S(2)}, u32[]{:S(2)}) async-start(f32[64,8,8,128]{3,2,1,0:T(8,128)} %flow_field.1), calls=%async_computation | async-start | bytes 4194304 | tf_op jit(solution)/shard_map/all_to_all | solution.py:357
  90.7 6.9 %collective-permute-start.4 = (f32[4,4,8,128]{3,2,1,0:T(8,128)}, f32[4,4,8,128]{3,2,1,0:T(8,128)S(1)}, u32[]{:S(2)}, u32[]{:S(2)}) collective-permute-start(f32[4,4,8,128]{3,2,1,0:T(8,128)} %get-tuple-element.15), channel_id=1, source_target_pairs={{0,3},{1,0},{2,1},{3,2},{4,7},{5,4},{6,5},{7,6},{8,11},{9,8},{10,9... | collective-permute-start | bytes 196616 | tf_op jit(solution)/shard_map/ppermute | solution.py:426
  91.2 6.4 %collective-permute-start.3 = (f32[4,4,8,128]{3,2,1,0:T(8,128)}, f32[4,4,8,128]{3,2,1,0:T(8,128)S(1)}, u32[]{:S(2)}, u32[]{:S(2)}) collective-permute-start(f32[4,4,8,128]{3,2,1,0:T(8,128)} %get-tuple-element.15), channel_id=1, source_target_pairs={{0,2},{1,3},{2,0},{3,1},{4,6},{5,7},{6,4},{7,5},{8,10},{9,11},{10,... | collective-permute-start | bytes 196616 | tf_op jit(solution)/shard_map/ppermute | solution.py:426
  93.8 4.5 %collective-permute-start.2 = (f32[4,4,8,128]{3,2,1,0:T(8,128)}, f32[4,4,8,128]{3,2,1,0:T(8,128)S(1)}, u32[]{:S(2)}, u32[]{:S(2)}) collective-permute-start(f32[4,4,8,128]{3,2,1,0:T(8,128)} %get-tuple-element.15), channel_id=1, source_target_pairs={{0,1},{1,2},{2,3},{3,0},{4,5},{5,6},{6,7},{7,4},{8,9},{9,10},{10,1... | collective-permute-start | bytes 196616 | tf_op jit(solution)/shard_map/ppermute | solution.py:426
  125.7 1.6 copy-start
  127.3 1.6 copy-start.2
  128.9 1.6 copy-start.7
  130.5 1.4 copy-start.8
  131.9 9.2 %copy-start.4 = (f32[128,4,8,128]{3,2,1,0:T(8,128)S(1)}, f32[128,4,8,128]{3,2,1,0:T(8,128)}, u32[]{:S(2)}) copy-start(f32[128,4,8,128]{3,2,1,0:T(8,128)} %get-tuple-element.20.inv_hbm) | copy-start | bytes 6291460
  131.9 9.2 %copy-start.5 = (f32[128,4,8,128]{3,2,1,0:T(8,128)S(1)}, f32[128,4,8,128]{3,2,1,0:T(8,128)}, u32[]{:S(2)}) copy-start(f32[128,4,8,128]{3,2,1,0:T(8,128)} %get-tuple-element.21.m_hbm) | copy-start | bytes 6291460
  131.9 9.2 %copy-start.6 = (f32[128,4,8,128]{3,2,1,0:T(8,128)S(1)}, f32[128,4,8,128]{3,2,1,0:T(8,128)}, u32[]{:S(2)}) copy-start(f32[128,4,8,128]{3,2,1,0:T(8,128)} %get-tuple-element.22.r_hbm) | copy-start | bytes 6291460
  136.1 9.2 %collective-permute-start.7 = (f32[2,4,8,128]{3,2,1,0:T(8,128)S(1)}, f32[2,4,8,128]{3,2,1,0:T(8,128)S(1)}, u32[]{:S(2)}, u32[]{:S(2)}) collective-permute-start(f32[2,4,8,128]{3,2,1,0:T(8,128)S(1)} %get-tuple-element.23.refs_0_), channel_id=1, source_target_pairs={{0,3},{1,0},{2,1},{3,2},{4,7},{5,4},{6,5},{7,6},{8,11},{9,8},{10,9... | collective-permute-start | bytes 98312 | tf_op jit(solution)/shard_map/ppermute | solution.py:467
  136.6 8.7 %collective-permute-start.6 = (f32[2,4,8,128]{3,2,1,0:T(8,128)S(1)}, f32[2,4,8,128]{3,2,1,0:T(8,128)S(1)}, u32[]{:S(2)}, u32[]{:S(2)}) collective-permute-start(f32[2,4,8,128]{3,2,1,0:T(8,128)S(1)} %get-tuple-element.23.refs_0_), channel_id=1, source_target_pairs={{0,2},{1,3},{2,0},{3,1},{4,6},{5,7},{6,4},{7,5},{8,10},{9,11},{10,... | collective-permute-start | bytes 98312 | tf_op jit(solution)/shard_map/ppermute | solution.py:467
  139.2 6.1 %collective-permute-start.5 = (f32[2,4,8,128]{3,2,1,0:T(8,128)S(1)}, f32[2,4,8,128]{3,2,1,0:T(8,128)S(1)}, u32[]{:S(2)}, u32[]{:S(2)}) collective-permute-start(f32[2,4,8,128]{3,2,1,0:T(8,128)S(1)} %get-tuple-element.23.refs_0_), channel_id=1, source_target_pairs={{0,1},{1,2},{2,3},{3,0},{4,5},{5,6},{6,7},{7,4},{8,9},{9,10},{10,1... | collective-permute-start | bytes 98312 | tf_op jit(solution)/shard_map/ppermute | solution.py:467
  141.1 4.2 %copy-start.1 = (f32[4,1024,128]{2,1,0:T(8,128)S(1)}, f32[4,1024,128]{2,1,0:T(8,128)}, u32[]{:S(2)}) copy-start(f32[4,1024,128]{2,1,0:T(8,128)} %get-tuple-element.17.v_hbm.refs_5_) | copy-start | bytes 6291460
  141.1 4.2 %copy-start.3 = (f32[4,1024,128]{2,1,0:T(8,128)S(1)}, f32[4,1024,128]{2,1,0:T(8,128)}, u32[]{:S(2)}) copy-start(f32[4,1024,128]{2,1,0:T(8,128)} %get-tuple-element.18.w_hbm.refs_6_) | copy-start | bytes 6291460
  141.1 4.2 %copy-start.9 = (bf16[512,1536]{1,0:T(8,128)(2,1)S(1)}, bf16[512,1536]{1,0:T(8,128)(2,1)}, u32[]{:S(2)}) copy-start(bf16[512,1536]{1,0:T(8,128)(2,1)} %constant.47.clone.refs_7_.t_ref) | copy-start | bytes 4718596

commit v2 on v1

--- a/solution.py
+++ b/solution.py
@@ -26,8 +26,15 @@
     scale = np.where(index >= 2, kappa, 0.0)[None, :]
     derive = np.where(odd_high, np.cos(angle), np.sin(angle)) * scale
     weight = np.where(index >= 2, 2.0, 1.0) / length
-    inverse = (forward * weight[None, :]).T
-    return forward, derive, inverse, (kappa * kappa).astype(np.float32)
+    inverse = forward * weight[None, :]
+    order = np.argsort(wave % 2, kind="stable")
+    square = (kappa * kappa).astype(np.float32)
+    return forward[:, order], derive[:, order], inverse[:, order], square[order]
+
+
+def halved(table):
+    half = table.shape[0] // 2
+    return table[:half, :half], table[:half, half:]
 
 
 def split_np(table):
@@ -36,14 +43,21 @@
     return high, low
 
 
-def left_table(table):
+def thrice(table, axis):
     high, low = split_np(table)
-    return np.concatenate([high, low, high], axis=1)
-
-
-def right_table(table):
-    high, low = split_np(table)
-    return np.concatenate([high, low, high], axis=0)
+    return np.concatenate([high, low, high], axis=axis)
+
+
+def slots_left(table):
+    return np.stack([thrice(part.T, 1) for part in halved(table)])
+
+
+def slots_right(table):
+    return np.stack([thrice(part, 0) for part in halved(table)])
+
+
+def nodes_left(table):
+    return np.stack([thrice(part, 1) for part in halved(table)])
 
 
 def parts(x, axis):
@@ -52,6 +66,21 @@
     return jnp.concatenate([high, high, low], axis=axis)
 
 
+def folded(x, axis):
+    half = x.shape[axis] // 2
+    first = lax.slice_in_dim(x, 0, half, axis=axis)
+    second = lax.slice_in_dim(x, half, 2 * half, axis=axis)
+    return parts(first + second, axis), parts(first - second, axis)
+
+
+def to_nodes(even, odd):
+    return jnp.concatenate([even + odd, even - odd], axis=0)
+
+
+def dot(a, b):
+    return jnp.dot(a, b, preferred_element_type=f32)
+
+
 def params(mib):
     return pltpu.CompilerParams(vmem_limit_bytes=mib * 1024 * 1024)
 
@@ -62,10 +91,15 @@
 
 def span_field_kernel(w_ref, t_ref, o_ref):
     x = jnp.concatenate([w_ref[0, 0], w_ref[0, 1]], axis=1)
-    y = jnp.dot(t_ref[...], parts(x, 0), preferred_element_type=f32)
+    for k, part in enumerate(folded(x, 0)):
+        store_modes(o_ref, k, dot(t_ref[k], part))
+
+
+def store_modes(o_ref, k, y):
+    owners = y.shape[0] // 8
     for p in range(2):
-        part = y[:, 128 * p : 128 * (p + 1)]
-        o_ref[:, p] = part.reshape(part.shape[0] // 8, 8, 128)
+        part = y[:, 128 * p : 128 * (p + 1)].reshape(owners, 8, 128)
+        o_ref[k * owners : (k + 1) * owners, p] = part
 
 
 def flow_field_kernel(u_ref, v_ref, before_ref, after_ref, width_ref, t_ref, o_ref):
@@ -83,14 +117,11 @@
         slopes.append((up - down) / width)
     u = jnp.concatenate([u_ref[0, 0], u_ref[0, 1]], axis=1)
     s = jnp.concatenate(slopes, axis=1)
-    x = jnp.concatenate([parts(u, 0), parts(s, 0)], axis=0)
-    y = jnp.dot(t_ref[...], x, preferred_element_type=f32)
-    for p in range(2):
-        part = y[:, 128 * p : 128 * (p + 1)]
-        o_ref[:, p] = part.reshape(part.shape[0] // 8, 8, 128)
-
-
-def factor_kernel(low_ref, up_ref, sigma_ref, inv_ref, m_ref, r_ref, v_ref, w_ref, ends_ref):
+    for k, pair in enumerate(zip(folded(u, 0), folded(s, 0))):
+        store_modes(o_ref, k, dot(t_ref[k], jnp.concatenate(pair, axis=0)))
+
+
+def factor_kernel(low_ref, up_ref, sigma_ref, inv_ref, v_ref, w_ref, ends_ref):
     rows = inv_ref.shape[0]
     tiles = inv_ref.shape[1]
 
@@ -100,16 +131,11 @@
         out = []
         for t in range(tiles):
             r, val = carry[t]
-            pivot = -(low + up) - sigma_ref[t] - low * r
-            inv = 1.0 / pivot
-            r = up * inv
-            m = low * inv
-            val = -m * val
+            inv = 1.0 / (-(low + up) - sigma_ref[t] - low * r)
+            val = -(low * inv) * val
             inv_ref[y, t] = inv
-            m_ref[y, t] = m
-            r_ref[y, t] = r
             v_ref[t, pl.ds(y, 8, stride=rows), :] = val
-            out.append((r, val))
+            out.append((up * inv, val))
         return tuple(out)
 
     zero = jnp.zeros((8, 128), f32)
@@ -121,7 +147,7 @@
         out = []
         for t in range(tiles):
             v, w = carry[t]
-            r = r_ref[y, t]
+            r = up_ref[y] * inv_ref[y, t]
             v = v_ref[t, pl.ds(y, 8, stride=rows), :] - r * v
             w = -r * w
             v_ref[t, pl.ds(y, 8, stride=rows), :] = v
@@ -137,19 +163,19 @@
         ends_ref[3, t] = w_ref[t, pl.ds(rows - 1, 8, stride=rows), :]
 
 
-def span_modes(x_ref, table, mode):
+def span_modes(x_ref, t_ref, mode):
     planes = x_ref.shape[0] // 8
     both = [
         jnp.transpose(x_ref[pl.ds(mode + p, planes, stride=8), :]) for p in range(2)
     ]
     x = jnp.concatenate(both, axis=0)
-    return jnp.dot(parts(x, 1), table, preferred_element_type=f32)
+    return jnp.concatenate([dot(part, t_ref[k]) for k, part in enumerate(folded(x, 1))], axis=1)
 
 
 def span_first_kernel(x_ref, t_ref, o_ref):
     tiles = o_ref.shape[0]
     for mode in range(0, 8, 2):
-        y = span_modes(x_ref, t_ref[...], mode)
+        y = span_modes(x_ref, t_ref, mode)
         for t in range(tiles):
             o_ref[t, mode * 128 : (mode + 2) * 128, :] = y[:, t * 128 : (t + 1) * 128]
 
@@ -183,7 +209,7 @@
     table.wait()
     weight = weight_ref[...]
     for pair in range(4):
-        y = span_modes(x_ref, t[...], 2 * pair)
+        y = span_modes(x_ref, t, 2 * pair)
         for copy in copies[pair]:
             copy.wait()
         for p in range(2):
@@ -202,34 +228,29 @@
                 )
 
 
-def sweep_kernel(x_ref, inv_hbm, m_hbm, r_hbm, o_ref, inv, m, r, held, sems):
+def sweep_kernel(low_ref, up_ref, x_ref, inv_hbm, o_ref, inv, held, sems):
     tiles = o_ref.shape[0]
     rows = inv.shape[0]
     count = 4
     chunk = rows // count
-
-    def copies(hbm, here, first):
-        return [
-            pltpu.make_async_copy(
-                hbm.at[pl.ds(c * chunk, chunk)], here.at[pl.ds(c * chunk, chunk)], sems.at[first + c]
-            )
-            for c in range(count)
-        ]
-
-    invs, ms, rs = copies(inv_hbm, inv, 0), copies(m_hbm, m, count), copies(r_hbm, r, 2 * count)
-    for c in range(count):
-        invs[c].start()
-        ms[c].start()
-    for c in range(count - 1, -1, -1):
-        rs[c].start()
+    copies = [
+        pltpu.make_async_copy(
+            inv_hbm.at[pl.ds(c * chunk, chunk)], inv.at[pl.ds(c * chunk, chunk)], sems.at[c]
+        )
+        for c in range(count)
+    ]
+    for copy in copies:
+        copy.start()
 
     def ahead(block, carry):
         for j in range(8):
             y = block * 8 + j
+            low = low_ref[y]
             out = []
             for t in range(tiles):
+                scale = inv[y, t]
                 side = x_ref[t, pl.ds(y, 8, stride=rows), :]
-                val = side * inv[y, t] - m[y, t] * carry[t]
+                val = side * scale - (low * scale) * carry[t]
                 held[y, t] = val
                 out.append(val)
             carry = tuple(out)
@@ -237,25 +258,22 @@
 
     carry = (jnp.zeros((8, 128), f32),) * tiles
     for c in range(count):
-        invs[c].wait()
-        ms[c].wait()
+        copies[c].wait()
         carry = lax.fori_loop(c * chunk // 8, (c + 1) * chunk // 8, ahead, carry)
 
     def back(step, carry):
         for j in range(8):
             y = rows - 1 - (step * 8 + j)
+            up = up_ref[y]
             out = []
             for t in range(tiles):
-                val = held[y, t] - r[y, t] * carry[t]
+                val = held[y, t] - (up * inv[y, t]) * carry[t]
                 o_ref[t, pl.ds(y, 8, stride=rows), :] = val
                 out.append(val)
             carry = tuple(out)
         return carry
 
-    carry = (jnp.zeros((8, 128), f32),) * tiles
-    for c in range(count):
-        rs[count - 1 - c].wait()
-        carry = lax.fori_loop(c * chunk // 8, (c + 1) * chunk // 8, back, carry)
+    lax.fori_loop(0, rows // 8, back, (jnp.zeros((8, 128), f32),) * tiles)
 
 
 def join_kernel(me_ref, y_ref, *refs):
@@ -319,9 +337,17 @@
                     y_ref[tile, part, :] + v[tile, part, :] * left + w[tile, part, :] * right
                 )
             columns.append(jnp.concatenate(both, axis=0))
-        x = jnp.concatenate(columns, axis=1)
-        y = lax.dot_general(
-            t[...], parts(x, 1), (((1,), (1,)), ((), ())), preferred_element_type=f32
+        half = tiles // 2
+        y = to_nodes(
+            *(
+                lax.dot_general(
+                    t[k],
+                    parts(jnp.concatenate(columns[k * half : (k + 1) * half], axis=1), 1),
+                    (((1,), (1,)), ((), ())),
+                    preferred_element_type=f32,
+                )
+                for k in range(2)
+            )
         )
         for p in range(2):
             part = y[:, 128 * p : 128 * (p + 1)]
@@ -332,7 +358,8 @@
     slots = x_ref.shape[0] // 8
     plane = pl.program_id(0) * 2
     x = jnp.concatenate([x_ref[pl.ds(plane + p, slots, stride=8), :] for p in range(2)], axis=1)
-    y = jnp.dot(t_ref[...], parts(x, 0), preferred_element_type=f32)
+    half = slots // 2
+    y = to_nodes(*(dot(t_ref[k], parts(x[k * half : (k + 1) * half], 0)) for k in range(2)))
     for p in range(2):
         o_ref[p] = y[:, 128 * p : 128 * (p + 1)]
 
@@ -357,7 +384,7 @@
         return lax.all_to_all(x, both, split_axis=0, concat_axis=0, tiled=True)
 
     field_shape = jax.ShapeDtypeStruct((group, planes, modes, rows), f32)
-    table = jnp.asarray(left_table(flow_forward.T))
+    table = jnp.asarray(slots_left(flow_forward))
     plane_block = lambda c: pl.BlockSpec((1, 2, flow_length, rows), lambda i: (c, i, 0, 0))
     whole = lambda *shape: pl.BlockSpec(shape, lambda i: (0,) * len(shape))
     out_block = pl.BlockSpec((group, 2, modes, rows), lambda i: (0, i, 0, 0))
@@ -383,7 +410,7 @@
     lower = 2.0 / (width * gaps[:-1])
     upper = 2.0 / (width * gaps[1:])
     flow_table = jnp.asarray(
-        np.concatenate([left_table(flow_derive.T), left_table(flow_forward.T)], axis=1)
+        np.concatenate([slots_left(flow_derive), slots_left(flow_forward)], axis=2)
     )
     flow_sent = pl.pallas_call(
         flow_field_kernel,
@@ -411,20 +438,22 @@
     slab_shape = jax.ShapeDtypeStruct((tiles, modes * rows, 128), f32)
     vmem = pl.BlockSpec(memory_space=pltpu.VMEM)
     smem = pl.BlockSpec(memory_space=pltpu.SMEM)
-    inv, m, r, v_all, w_all, vw_ends = pl.pallas_call(
+    inv, v_all, w_all, vw_ends = pl.pallas_call(
         factor_kernel,
         in_specs=[smem, smem, vmem],
-        out_specs=[vmem] * 6,
-        out_shape=[step_shape] * 3
+        out_specs=[vmem] * 4,
+        out_shape=[step_shape]
         + [slab_shape] * 2
         + [jax.ShapeDtypeStruct((4, tiles, modes, 128), f32)],
         compiler_params=params(58),
-        cost_estimate=cost(field_flops, 5 * field_bytes),
+        cost_estimate=cost(field_flops, 3 * field_bytes),
         name="factor",
     )(lower, upper, sigma)
     rings = [[(i, (i + n) % blocks) for i in range(blocks)] for n in range(1, blocks)]
     vw = jnp.stack([vw_ends] + [lax.ppermute(vw_ends, "gy", ring) for ring in rings])
-    span_here, vw = lax.optimization_barrier((span_here, vw))
+    weight = jnp.broadcast_to((0.5 * width)[:, None], (rows, 128))
+    end_gaps = jnp.stack([gaps[0], gaps[rows]])
+    span_here, vw, weight, end_gaps = lax.optimization_barrier((span_here, vw, weight, end_gaps))
 
     flat = (span_length * modes, rows)
     hbm = pl.BlockSpec(memory_space=pltpu.HBM)
@@ -436,30 +465,28 @@
         compiler_params=params(58),
         cost_estimate=cost(field_flops, 2 * field_bytes),
         name="span_first",
-    )(span_here.reshape(flat), jnp.asarray(right_table(span_derive)))
+    )(span_here.reshape(flat), jnp.asarray(slots_right(span_derive)))
     slab = pltpu.VMEM(slab_shape.shape, f32)
-    weight = jnp.broadcast_to((0.5 * width)[:, None], (rows, 128))
-    end_gaps = jnp.stack([gaps[0], gaps[rows]])
     source, y_ends = pl.pallas_call(
         source_kernel,
         in_specs=[vmem, vmem, smem] + [hbm] * 4,
         out_specs=[vmem] * 2,
         out_shape=[slab_shape, jax.ShapeDtypeStruct((2, tiles, modes, 128), f32)],
         scratch_shapes=[
-            pltpu.VMEM((3 * span_length, span_length), bf16),
+            pltpu.VMEM((2, 3 * span_length // 2, span_length // 2), bf16),
             slab,
             slab,
             slab,
             pltpu.SemaphoreType.DMA((13,)),
         ],
-        compiler_params=params(32),
+        compiler_params=params(48),
         cost_estimate=cost(field_flops, 5 * field_bytes),
         name="source",
     )(
         flow_here.reshape(flat),
         weight,
         end_gaps,
-        jnp.asarray(right_table(span_forward)),
+        jnp.asarray(slots_right(span_forward)),
         span_source,
         v_all,
         w_all,
@@ -468,14 +495,14 @@
     step = pltpu.VMEM(step_shape.shape, f32)
     y_all = pl.pallas_call(
         sweep_kernel,
-        in_specs=[vmem] + [hbm] * 3,
+        in_specs=[smem, smem, vmem, hbm],
         out_specs=vmem,
         out_shape=slab_shape,
-        scratch_shapes=[step] * 4 + [pltpu.SemaphoreType.DMA((12,))],
+        scratch_shapes=[step] * 2 + [pltpu.SemaphoreType.DMA((4,))],
         compiler_params=params(32),
-        cost_estimate=cost(field_flops, 5 * field_bytes),
+        cost_estimate=cost(field_flops, 3 * field_bytes),
         name="sweep",
-    )(source, inv, m, r)
+    )(lower, upper, source, inv)
     end_shape = (blocks + 1, tiles, modes, 128)
     back_sent = pl.pallas_call(
         join_kernel,
@@ -488,7 +515,7 @@
             pltpu.VMEM(end_shape, f32),
             slab,
             slab,
-            pltpu.VMEM((span_length, 3 * span_length), bf16),
+            pltpu.VMEM((2, span_length // 2, 3 * span_length // 2), bf16),
             pltpu.SemaphoreType.DMA((9,)),
         ],
         compiler_params=params(32),
@@ -501,10 +528,10 @@
         vw,
         v_all,
         w_all,
-        jnp.asarray(left_table(span_inverse.T)),
+        jnp.asarray(nodes_left(span_inverse)),
     )
     back_here = moved(back_sent)
-    last_table = jnp.asarray(left_table(flow_inverse.T))
+    last_table = jnp.asarray(nodes_left(flow_inverse))
     return pl.pallas_call(
         flow_inverse_kernel,
         grid=(planes // 2,),

time: 211 us -> 201 us (0.953)
  Pallas kernels: 50.5 us -> 43 us
  local copies, waits for them, and re-layouts: 13.3 us -> 7.06 us
  waiting for transfers between devices: 52.1 us -> 55.9 us
    unnamed x29 -> x23, local copies, waits for them, and re-layouts: 8.77 us -> 2.59 us
    all_to_all x2, waiting for transfers between devices: 50.8 us -> 54.4 us  [moved(): return lax.all_to_all(x, both, split_axis=0, concat_axis=0, tiled=True)]
    pallas_call x1, Pallas kernels: 4.57 us -> 2.23 us  [local(): pl.pallas_call(join_kernel, in_specs=[smem] + [vmem] * (2 + blocks) + [hb...]
  transfers between devices with their start and end apart: 10 -> 10, of which waited for: 4 -> 4; matrix products, arithmetic and copies ran while one was open for 4% -> 4% of each run, Pallas kernels for 16% -> 14%
where the time goes in v2:
time: 201 us; the launch traced here: 200 us
  blocking collectives  56.5 us (28%)
  waiting for transfers between devices  55.9 us (28%)
  Pallas kernels  43 us (21%)
  starting transfers between devices  33.3 us (17%)
  local copies, waits for them, and re-layouts  7.06 us (4%)
  other arithmetic  4.07 us (2%)
    all_to_all x1, blocking collectives, moved(): return lax.all_to_all(x, both, split_axis=0, concat_axis=0, tiled=True)  56.5 us
    all_to_all x2, waiting for transfers between devices, moved(): return lax.all_to_all(x, both, split_axis=0, concat_axis=0, tiled=True)  54.4 us
    all_to_all x2, starting transfers between devices, moved(): return lax.all_to_all(x, both, split_axis=0, concat_axis=0, tiled=True)  17.5 us
    pallas_call x1, Pallas kernels, local(): pl.pallas_call(factor_kernel, in_specs=[smem, smem, vmem], out_specs=[vme...  13.3 us
    pallas_call x1, Pallas kernels, local(): pl.pallas_call(flow_field_kernel, grid=(planes // 2,), in_specs=[plane_bl...  7.13 us
    ppermute x3, starting transfers between devices, local(): ends = [y_ends] + [lax.ppermute(y_ends, 'gy', ring) for ring in rings]  5.01 us
    ppermute x3, starting transfers between devices, local(): lax.ppermute(vw_ends, 'gy', ring)  4.93 us
    pallas_call x1, Pallas kernels, local(): pl.pallas_call(span_field_kernel, grid=(planes // 2,), in_specs=[plane_bl...  4.81 us
  transfers between devices with their start and end apart: 10, of which 4 were waited for; matrix products, arithmetic and copies ran while one was open for 4% of the time, Pallas kernels for 14%

profile of v2, /device:TPU:8, one launch (start us, length us, event | category | flops | bytes accessed | tf_op | source)
XLA Modules:
  0.0 200.0 jit_solution(7162526647681110410)
XLA Ops:
  0.0 4.8 %span_field.1 = f32[64,8,8,128]{3,2,1,0:T(8,128)} custom-call(f32[3,8,512,128]{3,2,1,0:T(8,128)} %w_ref.1, bf16[2,256,768]{2,1,0:T(8,128)(2,1)} %constant.41.clone.t_ref), custom_call_target="tpu_custom_call" | custom-call | flops 1610612736 | bytes 4194304 | tf_op jit(solution)/shard_map/span_field/pallas_call | solution.py:391
  4.8 12.2 %all-to-all-start.1 = ((f32[64,8,8,128]{3,2,1,0:T(8,128)}), f32[64,8,8,128]{3,2,1,0:T(8,128)}, u32[]{:S(2)}, u32[]{:S(2)}) async-start(f32[64,8,8,128]{3,2,1,0:T(8,128)} %span_field.1), calls=%async_computation.1 | async-start | bytes 4194304 | tf_op jit(solution)/shard_map/all_to_all | solution.py:384
  17.0 1.6 slice-done
  18.6 2.0 copy.12
  20.6 0.7 slice_bitcast_fusion
  21.3 2.4 %collective-permute-start.1 = (f32[8,512]{1,0:T(8,128)S(1)}, f32[8,512]{1,0:T(8,128)S(1)}, u32[]{:S(2)}, u32[]{:S(2)}) collective-permute-start(f32[8,512]{1,0:T(8,128)S(1)} %get-tuple-element.27), channel_id=1, source_target_pairs={{1,0},{2,1},{3,2},{5,4},{6,5},{7,6},{9,8},{10,9},{11,10},{13,12},{... | collective-permute-start | bytes 49160 | tf_op jit(solution)/shard_map/ppermute | solution.py:407
  23.7 3.5 %collective-permute-start = (f32[8,512]{1,0:T(8,128)S(1)}, f32[8,512]{1,0:T(8,128)S(1)}, u32[]{:S(2)}, u32[]{:S(2)}) collective-permute-start(f32[8,512]{1,0:T(8,128)S(1)} %get-tuple-element.28), channel_id=1, source_target_pairs={{0,1},{1,2},{2,3},{4,5},{5,6},{6,7},{8,9},{9,10},{10,11},{12,13},{... | collective-permute-start | bytes 49160 | tf_op jit(solution)/shard_map/ppermute | solution.py:406
  27.2 0.8 dynamic_slice.6
  27.9 0.7 broadcast_multiply_fusion
  28.6 0.7 collective-permute-done.before_ref
  29.3 0.6 copy-done.8
  29.9 7.1 %flow_field.1 = f32[64,8,8,128]{3,2,1,0:T(8,128)} custom-call(f32[3,8,512,128]{3,2,1,0:T(8,128)} %w_ref.1, f32[3,8,512,128]{3,2,1,0:T(8,128)} %w_ref.1, f32[8,512]{1,0:T(8,128)} %copy-done.8, f32[8,512]{1,0:T(8,128)} %copy-done.7, f32[1,128]{1,0:T(1,128)} %bitcast.21, bf16[2,256,1536]{2,1,0:T(8,128)(2,1)} %constant.42.clone.t_ref), custom_call_target="tpu_custom_call" | custom-call | flops 3221225472 | bytes 6291456 | tf_op jit(solution)/shard_map/flow_field/pallas_call | solution.py:415
  37.0 31.2 %all-to-all-done.1 = f32[64,8,8,128]{3,2,1,0:T(8,128)} async-done(((f32[64,8,8,128]{3,2,1,0:T(8,128)}), f32[64,8,8,128]{3,2,1,0:T(8,128)}, u32[]{:S(2)}, u32[]{:S(2)}) %all-to-all-start.1) | async-done | bytes 2097184 | tf_op jit(solution)/shard_map/all_to_all | solution.py:384
  68.2 5.3 %all-to-all-start = ((f32[64,8,8,128]{3,2,1,0:T(8,128)}), f32[64,8,8,128]{3,2,1,0:T(8,128)S(1)}, u32[]{:S(2)}, u32[]{:S(2)}) async-start(f32[64,8,8,128]{3,2,1,0:T(8,128)} %flow_field.1), calls=%async_computation | async-start | bytes 4194304 | tf_op jit(solution)/shard_map/all_to_all | solution.py:384
  73.6 0.8 dynamic_slice.7
  74.3 0.6 multiply_divide_fusion
  74.9 0.7 broadcast_add_fusion.sigma_ref
  75.6 13.3 %factor.1 = (f32[128,4,8,128]{3,2,1,0:T(8,128)}, f32[4,1024,128]{2,1,0:T(8,128)}, f32[4,1024,128]{2,1,0:T(8,128)}, f32[4,4,8,128]{3,2,1,0:T(8,128)}) custom-call(f32[128]{0:T(128)} %get-tuple-element.30.low_ref, f32[128]{0:T(128)} %get-tuple-element.29.up_ref, f32[4,8,128]{2,1,0:T(8,128)} %broadcast_add_fusion.sigma_ref), custom_call_target="tpu_custom_call" | custom-call | flops 1610612736 | bytes 6291456 | tf_op jit(solution)/shard_map/factor/pallas_call | solution.py:441
  89.3 2.6 %collective-permute-start.3 = (f32[4,4,8,128]{3,2,1,0:T(8,128)}, f32[4,4,8,128]{3,2,1,0:T(8,128)S(1)}, u32[]{:S(2)}, u32[]{:S(2)}) collective-permute-start(f32[4,4,8,128]{3,2,1,0:T(8,128)} %get-tuple-element.15), channel_id=1, source_target_pairs={{0,2},{1,3},{2,0},{3,1},{4,6},{5,7},{6,4},{7,5},{8,10},{9,11},{10,... | collective-permute-start | bytes 196616 | tf_op jit(solution)/shard_map/ppermute | solution.py:453
  91.9 1.9 collective-permute-start.2
  94.3 1.3 pad_maximum_fusion.1.gap_ref
  95.6 0.7 collective-permute-done.2
  96.3 0.9 pad_maximum_fusion.refs_4_
  97.3 4.4 %span_first.1.s_hbm = f32[4,1024,128]{2,1,0:T(8,128)} custom-call(f32[4096,128]{1,0:T(8,128)} %bitcast.10.x_ref, bf16[2,768,256]{2,1,0:T(8,128)(2,1)} %constant.45.clone.t_ref), custom_call_target="tpu_custom_call" | custom-call | flops 1610612736 | bytes 4194304 | tf_op jit(solution)/shard_map/span_first/pallas_call | solution.py:460
  101.7 23.2 %all-to-all-done = f32[64,8,8,128]{3,2,1,0:T(8,128)S(1)} async-done(((f32[64,8,8,128]{3,2,1,0:T(8,128)}), f32[64,8,8,128]{3,2,1,0:T(8,128)S(1)}, u32[]{:S(2)}, u32[]{:S(2)}) %all-to-all-start) | async-done | bytes 2097184 | tf_op jit(solution)/shard_map/all_to_all | solution.py:384
  124.9 4.1 %source.1 = (f32[4,1024,128]{2,1,0:T(8,128)S(1)}, f32[2,4,8,128]{3,2,1,0:T(8,128)S(1)}) custom-call(f32[4096,128]{1,0:T(8,128)S(1)} %bitcast.14, f32[128,128]{1,0:T(8,128)S(1)} %broadcast_in_dim.2.weight_ref, f32[2]{0:T(128)S(1)} %pad_maximum_fusion.1.gap_ref, bf16[2,768,256]{2,1,0:T(8,128)(2,1)S(1)} %copy-done.4, f32[4,1024,128]{2,1,0:T(8,128)} %span_first.1.s_hbm, ...), custom_call_target="tpu_custom_call" | custom-call | flops 1610612736 | bytes 10485760 | tf_op jit(solution)/shard_map/source/pallas_call | solution.py:470
  129.6 2.6 %collective-permute-start.6 = (f32[2,4,8,128]{3,2,1,0:T(8,128)S(1)}, f32[2,4,8,128]{3,2,1,0:T(8,128)S(1)}, u32[]{:S(2)}, u32[]{:S(2)}) collective-permute-start(f32[2,4,8,128]{3,2,1,0:T(8,128)S(1)} %get-tuple-element.23.refs_0_), channel_id=1, source_target_pairs={{0,2},{1,3},{2,0},{3,1},{4,6},{5,7},{6,4},{7,5},{8,10},{9,11},{10,... | collective-permute-start | bytes 98312 | tf_op jit(solution)/shard_map/ppermute | solution.py:494
  132.2 1.9 collective-permute-start.5
  134.1 4.2 %sweep.1.y_ref = f32[4,1024,128]{2,1,0:T(8,128)S(1)} custom-call(f32[128]{0:T(128)S(1)} %copy-done.6, f32[128]{0:T(128)S(1)} %copy-done.5, f32[4,1024,128]{2,1,0:T(8,128)S(1)} %get-tuple-element.21.x_ref, f32[128,4,8,128]{3,2,1,0:T(8,128)S(1)} %copy-done.2), custom_call_target="tpu_custom_call" | custom-call | flops 1610612736 | bytes 6291456 | tf_op jit(solution)/shard_map/sweep/pallas_call | solution.py:496
  138.4 2.2 %join.1 = f32[64,8,8,128]{3,2,1,0:T(8,128)S(1)} custom-call(s32[1]{0:T(128)} %bitcast.me_ref, f32[4,1024,128]{2,1,0:T(8,128)S(1)} %sweep.1.y_ref, f32[2,4,8,128]{3,2,1,0:T(8,128)S(1)} %get-tuple-element.23.refs_0_, f32[2,4,8,128]{3,2,1,0:T(8,128)S(1)} %collective-permute-done.5.refs_1_, f32[2,4,8,128]{3,2,1,0:T(8,128)S(1)} %collective-permute-done.6.refs_2_, ...), custom_call_target="tpu_custom_call" | custom-call | flops 1610612736 | bytes 8388608 | tf_op jit(solution)/shard_map/join/pallas_call | solution.py:507
  140.6 56.5 %all_to_all.15 = f32[64,8,8,128]{3,2,1,0:T(8,128)S(1)} all-to-all(f32[64,8,8,128]{3,2,1,0:T(8,128)S(1)} %join.1), channel_id=1, replica_groups=mesh['gx'=8,'gz'=8,'gy'=4] {'gx','gz'}, dimensions={0} | all-to-all | bytes 4194304 | tf_op jit(solution)/shard_map/all_to_all | solution.py:384
  197.1 2.9 %flow_inverse.1 = f32[8,512,128]{2,1,0:T(8,128)} custom-call(f32[4096,128]{1,0:T(8,128)S(1)} %bitcast.15, bf16[2,256,768]{2,1,0:T(8,128)(2,1)S(1)} %copy-done.3), custom_call_target="tpu_custom_call" | custom-call | flops 1610612736 | bytes 4194304 | tf_op jit(solution)/shard_map/flow_inverse/pallas_call | solution.py:535
  (32 shorter events, 1.7 us)
Async XLA Ops:
  4.8 63.4 %all-to-all-start.1 = ((f32[64,8,8,128]{3,2,1,0:T(8,128)}), f32[64,8,8,128]{3,2,1,0:T(8,128)}, u32[]{:S(2)}, u32[]{:S(2)}) async-start(f32[64,8,8,128]{3,2,1,0:T(8,128)} %span_field.1), calls=%async_computation.1 | async-start | bytes 4194304 | tf_op jit(solution)/shard_map/all_to_all | solution.py:384
  17.0 1.6 slice-start
  21.3 7.3 %collective-permute-start.1 = (f32[8,512]{1,0:T(8,128)S(1)}, f32[8,512]{1,0:T(8,128)S(1)}, u32[]{:S(2)}, u32[]{:S(2)}) collective-permute-start(f32[8,512]{1,0:T(8,128)S(1)} %get-tuple-element.27), channel_id=1, source_target_pairs={{1,0},{2,1},{3,2},{5,4},{6,5},{7,6},{9,8},{10,9},{11,10},{13,12},{... | collective-permute-start | bytes 49160 | tf_op jit(solution)/shard_map/ppermute | solution.py:407
  23.7 5.6 %collective-permute-start = (f32[8,512]{1,0:T(8,128)S(1)}, f32[8,512]{1,0:T(8,128)S(1)}, u32[]{:S(2)}, u32[]{:S(2)}) collective-permute-start(f32[8,512]{1,0:T(8,128)S(1)} %get-tuple-element.28), channel_id=1, source_target_pairs={{0,1},{1,2},{2,3},{4,5},{5,6},{6,7},{8,9},{9,10},{10,11},{12,13},{... | collective-permute-start | bytes 49160 | tf_op jit(solution)/shard_map/ppermute | solution.py:406
  28.6 0.7 copy-start.7
  29.3 0.6 copy-start.8
  37.0 37.3 %copy-start.9 = (f32[128]{0:T(128)S(1)}, f32[128]{0:T(128)}, u32[]{:S(2)}) copy-start(f32[128]{0:T(128)} %get-tuple-element.26) | copy-start | bytes 1540
  37.0 37.9 %copy-start.10 = (f32[4,128]{1,0:T(4,128)S(1)}, f32[4,128]{1,0:T(4,128)}, u32[]{:S(2)}) copy-start(f32[4,128]{1,0:T(4,128)} %constant.49) | copy-start | bytes 6148
  68.2 56.7 %all-to-all-start = ((f32[64,8,8,128]{3,2,1,0:T(8,128)}), f32[64,8,8,128]{3,2,1,0:T(8,128)S(1)}, u32[]{:S(2)}, u32[]{:S(2)}) async-start(f32[64,8,8,128]{3,2,1,0:T(8,128)} %flow_field.1), calls=%async_computation | async-start | bytes 4194304 | tf_op jit(solution)/shard_map/all_to_all | solution.py:384
  88.8 6.8 %collective-permute-start.4 = (f32[4,4,8,128]{3,2,1,0:T(8,128)}, f32[4,4,8,128]{3,2,1,0:T(8,128)S(1)}, u32[]{:S(2)}, u32[]{:S(2)}) collective-permute-start(f32[4,4,8,128]{3,2,1,0:T(8,128)} %get-tuple-element.15), channel_id=1, source_target_pairs={{0,3},{1,0},{2,1},{3,2},{4,7},{5,4},{6,5},{7,6},{8,11},{9,8},{10,9... | collective-permute-start | bytes 196616 | tf_op jit(solution)/shard_map/ppermute | solution.py:453
  89.3 6.4 %collective-permute-start.3 = (f32[4,4,8,128]{3,2,1,0:T(8,128)}, f32[4,4,8,128]{3,2,1,0:T(8,128)S(1)}, u32[]{:S(2)}, u32[]{:S(2)}) collective-permute-start(f32[4,4,8,128]{3,2,1,0:T(8,128)} %get-tuple-element.15), channel_id=1, source_target_pairs={{0,2},{1,3},{2,0},{3,1},{4,6},{5,7},{6,4},{7,5},{8,10},{9,11},{10,... | collective-permute-start | bytes 196616 | tf_op jit(solution)/shard_map/ppermute | solution.py:453
  91.9 4.5 %collective-permute-start.2 = (f32[4,4,8,128]{3,2,1,0:T(8,128)}, f32[4,4,8,128]{3,2,1,0:T(8,128)S(1)}, u32[]{:S(2)}, u32[]{:S(2)}) collective-permute-start(f32[4,4,8,128]{3,2,1,0:T(8,128)} %get-tuple-element.15), channel_id=1, source_target_pairs={{0,1},{1,2},{2,3},{3,0},{4,5},{5,6},{6,7},{7,4},{8,9},{9,10},{10,1... | collective-permute-start | bytes 196616 | tf_op jit(solution)/shard_map/ppermute | solution.py:453
  97.3 27.7 %copy-start.4 = (bf16[2,768,256]{2,1,0:T(8,128)(2,1)S(1)}, bf16[2,768,256]{2,1,0:T(8,128)(2,1)}, u32[]{:S(2)}) copy-start(bf16[2,768,256]{2,1,0:T(8,128)(2,1)} %constant.46.clone.t_hbm) | copy-start | bytes 2359300
  124.9 9.2 %copy-start.2 = (f32[128,4,8,128]{3,2,1,0:T(8,128)S(1)}, f32[128,4,8,128]{3,2,1,0:T(8,128)}, u32[]{:S(2)}) copy-start(f32[128,4,8,128]{3,2,1,0:T(8,128)} %get-tuple-element.22.inv_hbm) | copy-start | bytes 6291460
  124.9 9.2 %copy-start.5 = (f32[128]{0:T(128)S(1)}, f32[128]{0:T(128)}, u32[]{:S(2)}) copy-start(f32[128]{0:T(128)} %get-tuple-element.29.up_ref) | copy-start | bytes 1540
  124.9 9.2 %copy-start.6 = (f32[128]{0:T(128)S(1)}, f32[128]{0:T(128)}, u32[]{:S(2)}) copy-start(f32[128]{0:T(128)} %get-tuple-element.30.low_ref) | copy-start | bytes 1540
  129.1 9.2 %collective-permute-start.7 = (f32[2,4,8,128]{3,2,1,0:T(8,128)S(1)}, f32[2,4,8,128]{3,2,1,0:T(8,128)S(1)}, u32[]{:S(2)}, u32[]{:S(2)}) collective-permute-start(f32[2,4,8,128]{3,2,1,0:T(8,128)S(1)} %get-tuple-element.23.refs_0_), channel_id=1, source_target_pairs={{0,3},{1,0},{2,1},{3,2},{4,7},{5,4},{6,5},{7,6},{8,11},{9,8},{10,9... | collective-permute-start | bytes 98312 | tf_op jit(solution)/shard_map/ppermute | solution.py:494
  129.6 8.7 %collective-permute-start.6 = (f32[2,4,8,128]{3,2,1,0:T(8,128)S(1)}, f32[2,4,8,128]{3,2,1,0:T(8,128)S(1)}, u32[]{:S(2)}, u32[]{:S(2)}) collective-permute-start(f32[2,4,8,128]{3,2,1,0:T(8,128)S(1)} %get-tuple-element.23.refs_0_), channel_id=1, source_target_pairs={{0,2},{1,3},{2,0},{3,1},{4,6},{5,7},{6,4},{7,5},{8,10},{9,11},{10,... | collective-permute-start | bytes 98312 | tf_op jit(solution)/shard_map/ppermute | solution.py:494
  132.2 6.1 %collective-permute-start.5 = (f32[2,4,8,128]{3,2,1,0:T(8,128)S(1)}, f32[2,4,8,128]{3,2,1,0:T(8,128)S(1)}, u32[]{:S(2)}, u32[]{:S(2)}) collective-permute-start(f32[2,4,8,128]{3,2,1,0:T(8,128)S(1)} %get-tuple-element.23.refs_0_), channel_id=1, source_target_pairs={{0,1},{1,2},{2,3},{3,0},{4,5},{5,6},{6,7},{7,4},{8,9},{9,10},{10,1... | collective-permute-start | bytes 98312 | tf_op jit(solution)/shard_map/ppermute | solution.py:494
  134.1 4.3 %copy-start = (f32[4,1024,128]{2,1,0:T(8,128)S(1)}, f32[4,1024,128]{2,1,0:T(8,128)}, u32[]{:S(2)}) copy-start(f32[4,1024,128]{2,1,0:T(8,128)} %get-tuple-element.19.v_hbm.refs_5_) | copy-start | bytes 6291460
  134.1 4.3 %copy-start.1 = (f32[4,1024,128]{2,1,0:T(8,128)S(1)}, f32[4,1024,128]{2,1,0:T(8,128)}, u32[]{:S(2)}) copy-start(f32[4,1024,128]{2,1,0:T(8,128)} %get-tuple-element.20.w_hbm.refs_6_) | copy-start | bytes 6291460
  134.1 4.3 %copy-start.3 = (bf16[2,256,768]{2,1,0:T(8,128)(2,1)S(1)}, bf16[2,256,768]{2,1,0:T(8,128)(2,1)}, u32[]{:S(2)}) copy-start(bf16[2,256,768]{2,1,0:T(8,128)(2,1)} %constant.47.clone.refs_7_.t_ref) | copy-start | bytes 2359300

commit v3 on v2

--- a/solution.py
+++ b/solution.py
@@ -89,10 +89,26 @@
     return pl.CostEstimate(flops=flops, bytes_accessed=size, transcendentals=0)
 
 
-def span_field_kernel(w_ref, t_ref, o_ref):
-    x = jnp.concatenate([w_ref[0, 0], w_ref[0, 1]], axis=1)
-    for k, part in enumerate(folded(x, 0)):
-        store_modes(o_ref, k, dot(t_ref[k], part))
+def span_field_kernel(w_hbm, t_hbm, o_hbm, w, t, o, sems):
+    loads, stores = [], []
+    for pair in range(4):
+        part = pl.ds(2 * pair, 2)
+        loads.append(pltpu.make_async_copy(w_hbm.at[2, part], w.at[part], sems.at[pair]))
+        stores.append(pltpu.make_async_copy(o.at[:, part], o_hbm.at[:, part], sems.at[4 + pair]))
+    tables = [pltpu.make_async_copy(t_hbm.at[k], t.at[k], sems.at[8 + k]) for k in range(2)]
+    loads[0].start()
+    for copy in tables + loads[1:]:
+        copy.start()
+    for pair in range(4):
+        loads[pair].wait()
+        x = jnp.concatenate([w[2 * pair], w[2 * pair + 1]], axis=1)
+        for k, part in enumerate(folded(x, 0)):
+            if pair == 0:
+                tables[k].wait()
+            store_modes(o.at[:, 2 * pair : 2 * pair + 2], k, dot(t[k], part))
+        stores[pair].start()
+    for copy in stores:
+        copy.wait()
 
 
 def store_modes(o_ref, k, y):
@@ -354,14 +370,21 @@
             o_ref[:, 2 * pair + p] = part.reshape(part.shape[0] // 8, 8, 128)
 
 
-def flow_inverse_kernel(x_ref, t_ref, o_ref):
+def flow_inverse_kernel(x_ref, t_ref, o_hbm, o, sems):
     slots = x_ref.shape[0] // 8
-    plane = pl.program_id(0) * 2
-    x = jnp.concatenate([x_ref[pl.ds(plane + p, slots, stride=8), :] for p in range(2)], axis=1)
     half = slots // 2
-    y = to_nodes(*(dot(t_ref[k], parts(x[k * half : (k + 1) * half], 0)) for k in range(2)))
-    for p in range(2):
-        o_ref[p] = y[:, 128 * p : 128 * (p + 1)]
+    stores = []
+    for pair in range(4):
+        plane = 2 * pair
+        x = jnp.concatenate([x_ref[pl.ds(plane + p, slots, stride=8), :] for p in range(2)], axis=1)
+        y = to_nodes(*(dot(t_ref[k], parts(x[k * half : (k + 1) * half], 0)) for k in range(2)))
+        for p in range(2):
+            o[plane + p] = y[:, 128 * p : 128 * (p + 1)]
+        part = pl.ds(plane, 2)
+        stores.append(pltpu.make_async_copy(o.at[part], o_hbm.at[part], sems.at[pair]))
+        stores[-1].start()
+    for copy in stores:
+        copy.wait()
 
 
 def local(velocity, spacing):
@@ -388,12 +411,18 @@
     plane_block = lambda c: pl.BlockSpec((1, 2, flow_length, rows), lambda i: (c, i, 0, 0))
     whole = lambda *shape: pl.BlockSpec(shape, lambda i: (0,) * len(shape))
     out_block = pl.BlockSpec((group, 2, modes, rows), lambda i: (0, i, 0, 0))
+    any_place = pl.BlockSpec(memory_space=pl.ANY)
     span_sent = pl.pallas_call(
         span_field_kernel,
-        grid=(planes // 2,),
-        in_specs=[plane_block(2), whole(*table.shape)],
-        out_specs=out_block,
+        in_specs=[any_place] * 2,
+        out_specs=any_place,
         out_shape=field_shape,
+        scratch_shapes=[
+            pltpu.VMEM((planes, flow_length, rows), f32),
+            pltpu.VMEM(table.shape, bf16),
+            pltpu.VMEM(field_shape.shape, f32),
+            pltpu.SemaphoreType.DMA((10,)),
+        ],
         compiler_params=params(58),
         cost_estimate=cost(field_flops, 2 * field_bytes),
         name="span_field",
@@ -534,10 +563,13 @@
     last_table = jnp.asarray(nodes_left(flow_inverse))
     return pl.pallas_call(
         flow_inverse_kernel,
-        grid=(planes // 2,),
-        in_specs=[whole(flow_length * planes, rows), whole(*last_table.shape)],
-        out_specs=pl.BlockSpec((2, flow_length, rows), lambda i: (i, 0, 0)),
+        in_specs=[vmem] * 2,
+        out_specs=any_place,
         out_shape=jax.ShapeDtypeStruct((planes, flow_length, rows), f32),
+        scratch_shapes=[
+            pltpu.VMEM((planes, flow_length, rows), f32),
+            pltpu.SemaphoreType.DMA((4,)),
+        ],
         compiler_params=params(32),
         cost_estimate=cost(field_flops, 2 * field_bytes),
         name="flow_inverse",

time: 201 us -> 199 us (0.990)
  transfers between devices with their start and end apart: 10 -> 10, of which waited for: 4 -> 4; matrix products, arithmetic and copies ran while one was open for 4% -> 4% of each run, Pallas kernels for 14% -> 15%
where the time goes in v3:
time: 199 us; the launch traced here: 198 us
  blocking collectives  56.5 us (28%)
  waiting for transfers between devices  55.9 us (28%)
  Pallas kernels  41.3 us (21%)
  starting transfers between devices  33.3 us (17%)
  local copies, waits for them, and re-layouts  7.06 us (4%)
  other arithmetic  4.07 us (2%)
    all_to_all x1, blocking collectives, moved(): return lax.all_to_all(x, both, split_axis=0, concat_axis=0, tiled=True)  56.5 us
    all_to_all x2, waiting for transfers between devices, moved(): return lax.all_to_all(x, both, split_axis=0, concat_axis=0, tiled=True)  54.4 us
    all_to_all x2, starting transfers between devices, moved(): return lax.all_to_all(x, both, split_axis=0, concat_axis=0, tiled=True)  17.5 us
    pallas_call x1, Pallas kernels, local(): pl.pallas_call(factor_kernel, in_specs=[smem, smem, vmem], out_specs=[vme...  13.3 us
    pallas_call x1, Pallas kernels, local(): pl.pallas_call(flow_field_kernel, grid=(planes // 2,), in_specs=[plane_bl...  7.13 us
    ppermute x3, starting transfers between devices, local(): ends = [y_ends] + [lax.ppermute(y_ends, 'gy', ring) for ring in rings]  5.01 us
    ppermute x3, starting transfers between devices, local(): lax.ppermute(vw_ends, 'gy', ring)  4.93 us
    pallas_call x1, Pallas kernels, local(): pl.pallas_call(span_first_kernel, in_specs=[vmem, vmem], out_specs=vmem,...  4.39 us
  transfers between devices with their start and end apart: 10, of which 4 were waited for; matrix products, arithmetic and copies ran while one was open for 4% of the time, Pallas kernels for 15%

profile of v3, /device:TPU:8, one launch (start us, length us, event | category | flops | bytes accessed | tf_op | source)
XLA Modules:
  0.0 198.5 jit_solution(3277324614337846019)
XLA Ops:
  0.0 4.0 %span_field.1 = f32[64,8,8,128]{3,2,1,0:T(8,128)} custom-call(f32[3,8,512,128]{3,2,1,0:T(8,128)} %w_hbm.1, bf16[2,256,768]{2,1,0:T(8,128)(2,1)} %constant.41.clone.t_hbm), custom_call_target="tpu_custom_call" | custom-call | flops 1610612736 | bytes 4194304 | tf_op jit(solution)/shard_map/span_field/pallas_call | solution.py:415
  4.0 12.2 %all-to-all-start.1 = ((f32[64,8,8,128]{3,2,1,0:T(8,128)}), f32[64,8,8,128]{3,2,1,0:T(8,128)}, u32[]{:S(2)}, u32[]{:S(2)}) async-start(f32[64,8,8,128]{3,2,1,0:T(8,128)} %span_field.1), calls=%async_computation.1 | async-start | bytes 4194304 | tf_op jit(solution)/shard_map/all_to_all | solution.py:407
  16.2 1.6 slice-done
  17.8 2.0 copy.12
  19.8 0.7 slice_bitcast_fusion
  20.5 2.4 %collective-permute-start.1 = (f32[8,512]{1,0:T(8,128)S(1)}, f32[8,512]{1,0:T(8,128)S(1)}, u32[]{:S(2)}, u32[]{:S(2)}) collective-permute-start(f32[8,512]{1,0:T(8,128)S(1)} %get-tuple-element.27), channel_id=1, source_target_pairs={{1,0},{2,1},{3,2},{5,4},{6,5},{7,6},{9,8},{10,9},{11,10},{13,12},{... | collective-permute-start | bytes 49160 | tf_op jit(solution)/shard_map/ppermute | solution.py:436
  22.9 3.5 %collective-permute-start = (f32[8,512]{1,0:T(8,128)S(1)}, f32[8,512]{1,0:T(8,128)S(1)}, u32[]{:S(2)}, u32[]{:S(2)}) collective-permute-start(f32[8,512]{1,0:T(8,128)S(1)} %get-tuple-element.28), channel_id=1, source_target_pairs={{0,1},{1,2},{2,3},{4,5},{5,6},{6,7},{8,9},{9,10},{10,11},{12,13},{... | collective-permute-start | bytes 49160 | tf_op jit(solution)/shard_map/ppermute | solution.py:435
  26.3 0.8 dynamic_slice.6
  27.1 0.7 broadcast_multiply_fusion
  27.8 0.7 collective-permute-done.before_ref
  28.5 0.6 copy-done.8
  29.1 7.1 %flow_field.1 = f32[64,8,8,128]{3,2,1,0:T(8,128)} custom-call(f32[3,8,512,128]{3,2,1,0:T(8,128)} %w_hbm.1, f32[3,8,512,128]{3,2,1,0:T(8,128)} %w_hbm.1, f32[8,512]{1,0:T(8,128)} %copy-done.8, f32[8,512]{1,0:T(8,128)} %copy-done.7, f32[1,128]{1,0:T(1,128)} %bitcast.21, bf16[2,256,1536]{2,1,0:T(8,128)(2,1)} %constant.42.clone.t_ref), custom_call_target="tpu_custom_call" | custom-call | flops 3221225472 | bytes 6291456 | tf_op jit(solution)/shard_map/flow_field/pallas_call | solution.py:444
  36.2 31.2 %all-to-all-done.1 = f32[64,8,8,128]{3,2,1,0:T(8,128)} async-done(((f32[64,8,8,128]{3,2,1,0:T(8,128)}), f32[64,8,8,128]{3,2,1,0:T(8,128)}, u32[]{:S(2)}, u32[]{:S(2)}) %all-to-all-start.1) | async-done | bytes 2097184 | tf_op jit(solution)/shard_map/all_to_all | solution.py:407
  67.4 5.3 %all-to-all-start = ((f32[64,8,8,128]{3,2,1,0:T(8,128)}), f32[64,8,8,128]{3,2,1,0:T(8,128)S(1)}, u32[]{:S(2)}, u32[]{:S(2)}) async-start(f32[64,8,8,128]{3,2,1,0:T(8,128)} %flow_field.1), calls=%async_computation | async-start | bytes 4194304 | tf_op jit(solution)/shard_map/all_to_all | solution.py:407
  72.7 0.8 dynamic_slice.7
  73.5 0.6 multiply_divide_fusion
  74.1 0.7 broadcast_add_fusion.sigma_ref
  74.7 13.3 %factor.1 = (f32[128,4,8,128]{3,2,1,0:T(8,128)}, f32[4,1024,128]{2,1,0:T(8,128)}, f32[4,1024,128]{2,1,0:T(8,128)}, f32[4,4,8,128]{3,2,1,0:T(8,128)}) custom-call(f32[128]{0:T(128)} %get-tuple-element.30.low_ref, f32[128]{0:T(128)} %get-tuple-element.29.up_ref, f32[4,8,128]{2,1,0:T(8,128)} %broadcast_add_fusion.sigma_ref), custom_call_target="tpu_custom_call" | custom-call | flops 1610612736 | bytes 6291456 | tf_op jit(solution)/shard_map/factor/pallas_call | solution.py:470
  88.5 2.6 %collective-permute-start.3 = (f32[4,4,8,128]{3,2,1,0:T(8,128)}, f32[4,4,8,128]{3,2,1,0:T(8,128)S(1)}, u32[]{:S(2)}, u32[]{:S(2)}) collective-permute-start(f32[4,4,8,128]{3,2,1,0:T(8,128)} %get-tuple-element.15), channel_id=1, source_target_pairs={{0,2},{1,3},{2,0},{3,1},{4,6},{5,7},{6,4},{7,5},{8,10},{9,11},{10,... | collective-permute-start | bytes 196616 | tf_op jit(solution)/shard_map/ppermute | solution.py:482
  91.0 1.9 collective-permute-start.2
  93.5 1.3 pad_maximum_fusion.1.gap_ref
  94.8 0.7 collective-permute-done.2
  95.5 0.9 pad_maximum_fusion.refs_4_
  96.5 4.4 %span_first.1.s_hbm = f32[4,1024,128]{2,1,0:T(8,128)} custom-call(f32[4096,128]{1,0:T(8,128)} %bitcast.10.x_ref, bf16[2,768,256]{2,1,0:T(8,128)(2,1)} %constant.45.clone.t_ref), custom_call_target="tpu_custom_call" | custom-call | flops 1610612736 | bytes 4194304 | tf_op jit(solution)/shard_map/span_first/pallas_call | solution.py:489
  100.9 23.2 %all-to-all-done = f32[64,8,8,128]{3,2,1,0:T(8,128)S(1)} async-done(((f32[64,8,8,128]{3,2,1,0:T(8,128)}), f32[64,8,8,128]{3,2,1,0:T(8,128)S(1)}, u32[]{:S(2)}, u32[]{:S(2)}) %all-to-all-start) | async-done | bytes 2097184 | tf_op jit(solution)/shard_map/all_to_all | solution.py:407
  124.1 4.1 %source.1 = (f32[4,1024,128]{2,1,0:T(8,128)S(1)}, f32[2,4,8,128]{3,2,1,0:T(8,128)S(1)}) custom-call(f32[4096,128]{1,0:T(8,128)S(1)} %bitcast.14, f32[128,128]{1,0:T(8,128)S(1)} %broadcast_in_dim.2.weight_ref, f32[2]{0:T(128)S(1)} %pad_maximum_fusion.1.gap_ref, bf16[2,768,256]{2,1,0:T(8,128)(2,1)S(1)} %copy-done.4, f32[4,1024,128]{2,1,0:T(8,128)} %span_first.1.s_hbm, ...), custom_call_target="tpu_custom_call" | custom-call | flops 1610612736 | bytes 10485760 | tf_op jit(solution)/shard_map/source/pallas_call | solution.py:499
  128.8 2.6 %collective-permute-start.6 = (f32[2,4,8,128]{3,2,1,0:T(8,128)S(1)}, f32[2,4,8,128]{3,2,1,0:T(8,128)S(1)}, u32[]{:S(2)}, u32[]{:S(2)}) collective-permute-start(f32[2,4,8,128]{3,2,1,0:T(8,128)S(1)} %get-tuple-element.23.refs_0_), channel_id=1, source_target_pairs={{0,2},{1,3},{2,0},{3,1},{4,6},{5,7},{6,4},{7,5},{8,10},{9,11},{10,... | collective-permute-start | bytes 98312 | tf_op jit(solution)/shard_map/ppermute | solution.py:523
  131.4 1.9 collective-permute-start.5
  133.3 4.2 %sweep.1.y_ref = f32[4,1024,128]{2,1,0:T(8,128)S(1)} custom-call(f32[128]{0:T(128)S(1)} %copy-done.6, f32[128]{0:T(128)S(1)} %copy-done.5, f32[4,1024,128]{2,1,0:T(8,128)S(1)} %get-tuple-element.21.x_ref, f32[128,4,8,128]{3,2,1,0:T(8,128)S(1)} %copy-done.2), custom_call_target="tpu_custom_call" | custom-call | flops 1610612736 | bytes 6291456 | tf_op jit(solution)/shard_map/sweep/pallas_call | solution.py:525
  137.6 2.2 %join.1 = f32[64,8,8,128]{3,2,1,0:T(8,128)S(1)} custom-call(s32[1]{0:T(128)} %bitcast.me_ref, f32[4,1024,128]{2,1,0:T(8,128)S(1)} %sweep.1.y_ref, f32[2,4,8,128]{3,2,1,0:T(8,128)S(1)} %get-tuple-element.23.refs_0_, f32[2,4,8,128]{3,2,1,0:T(8,128)S(1)} %collective-permute-done.5.refs_1_, f32[2,4,8,128]{3,2,1,0:T(8,128)S(1)} %collective-permute-done.6.refs_2_, ...), custom_call_target="tpu_custom_call" | custom-call | flops 1610612736 | bytes 8388608 | tf_op jit(solution)/shard_map/join/pallas_call | solution.py:536
  139.8 56.5 %all_to_all.15 = f32[64,8,8,128]{3,2,1,0:T(8,128)S(1)} all-to-all(f32[64,8,8,128]{3,2,1,0:T(8,128)S(1)} %join.1), channel_id=1, replica_groups=mesh['gx'=8,'gz'=8,'gy'=4] {'gx','gz'}, dimensions={0} | all-to-all | bytes 4194304 | tf_op jit(solution)/shard_map/all_to_all | solution.py:407
  196.3 2.0 %flow_inverse.1 = f32[8,512,128]{2,1,0:T(8,128)} custom-call(f32[4096,128]{1,0:T(8,128)S(1)} %bitcast.15, bf16[2,256,768]{2,1,0:T(8,128)(2,1)S(1)} %copy-done.3), custom_call_target="tpu_custom_call" | custom-call | flops 1610612736 | bytes 4194304 | tf_op jit(solution)/shard_map/flow_inverse/pallas_call | solution.py:564
  (32 shorter events, 1.7 us)
Async XLA Ops:
  4.0 63.4 %all-to-all-start.1 = ((f32[64,8,8,128]{3,2,1,0:T(8,128)}), f32[64,8,8,128]{3,2,1,0:T(8,128)}, u32[]{:S(2)}, u32[]{:S(2)}) async-start(f32[64,8,8,128]{3,2,1,0:T(8,128)} %span_field.1), calls=%async_computation.1 | async-start | bytes 4194304 | tf_op jit(solution)/shard_map/all_to_all | solution.py:407
  16.2 1.6 slice-start
  20.5 7.3 %collective-permute-start.1 = (f32[8,512]{1,0:T(8,128)S(1)}, f32[8,512]{1,0:T(8,128)S(1)}, u32[]{:S(2)}, u32[]{:S(2)}) collective-permute-start(f32[8,512]{1,0:T(8,128)S(1)} %get-tuple-element.27), channel_id=1, source_target_pairs={{1,0},{2,1},{3,2},{5,4},{6,5},{7,6},{9,8},{10,9},{11,10},{13,12},{... | collective-permute-start | bytes 49160 | tf_op jit(solution)/shard_map/ppermute | solution.py:436
  22.9 5.6 %collective-permute-start = (f32[8,512]{1,0:T(8,128)S(1)}, f32[8,512]{1,0:T(8,128)S(1)}, u32[]{:S(2)}, u32[]{:S(2)}) collective-permute-start(f32[8,512]{1,0:T(8,128)S(1)} %get-tuple-element.28), channel_id=1, source_target_pairs={{0,1},{1,2},{2,3},{4,5},{5,6},{6,7},{8,9},{9,10},{10,11},{12,13},{... | collective-permute-start | bytes 49160 | tf_op jit(solution)/shard_map/ppermute | solution.py:435
  27.8 0.7 copy-start.7
  28.5 0.6 copy-start.8
  36.2 37.3 %copy-start.9 = (f32[128]{0:T(128)S(1)}, f32[128]{0:T(128)}, u32[]{:S(2)}) copy-start(f32[128]{0:T(128)} %get-tuple-element.26) | copy-start | bytes 1540
  36.2 37.9 %copy-start.10 = (f32[4,128]{1,0:T(4,128)S(1)}, f32[4,128]{1,0:T(4,128)}, u32[]{:S(2)}) copy-start(f32[4,128]{1,0:T(4,128)} %constant.49) | copy-start | bytes 6148
  67.4 56.7 %all-to-all-start = ((f32[64,8,8,128]{3,2,1,0:T(8,128)}), f32[64,8,8,128]{3,2,1,0:T(8,128)S(1)}, u32[]{:S(2)}, u32[]{:S(2)}) async-start(f32[64,8,8,128]{3,2,1,0:T(8,128)} %flow_field.1), calls=%async_computation | async-start | bytes 4194304 | tf_op jit(solution)/shard_map/all_to_all | solution.py:407
  88.0 6.8 %collective-permute-start.4 = (f32[4,4,8,128]{3,2,1,0:T(8,128)}, f32[4,4,8,128]{3,2,1,0:T(8,128)S(1)}, u32[]{:S(2)}, u32[]{:S(2)}) collective-permute-start(f32[4,4,8,128]{3,2,1,0:T(8,128)} %get-tuple-element.15), channel_id=1, source_target_pairs={{0,3},{1,0},{2,1},{3,2},{4,7},{5,4},{6,5},{7,6},{8,11},{9,8},{10,9... | collective-permute-start | bytes 196616 | tf_op jit(solution)/shard_map/ppermute | solution.py:482
  88.5 6.4 %collective-permute-start.3 = (f32[4,4,8,128]{3,2,1,0:T(8,128)}, f32[4,4,8,128]{3,2,1,0:T(8,128)S(1)}, u32[]{:S(2)}, u32[]{:S(2)}) collective-permute-start(f32[4,4,8,128]{3,2,1,0:T(8,128)} %get-tuple-element.15), channel_id=1, source_target_pairs={{0,2},{1,3},{2,0},{3,1},{4,6},{5,7},{6,4},{7,5},{8,10},{9,11},{10,... | collective-permute-start | bytes 196616 | tf_op jit(solution)/shard_map/ppermute | solution.py:482
  91.0 4.5 %collective-permute-start.2 = (f32[4,4,8,128]{3,2,1,0:T(8,128)}, f32[4,4,8,128]{3,2,1,0:T(8,128)S(1)}, u32[]{:S(2)}, u32[]{:S(2)}) collective-permute-start(f32[4,4,8,128]{3,2,1,0:T(8,128)} %get-tuple-element.15), channel_id=1, source_target_pairs={{0,1},{1,2},{2,3},{3,0},{4,5},{5,6},{6,7},{7,4},{8,9},{9,10},{10,1... | collective-permute-start | bytes 196616 | tf_op jit(solution)/shard_map/ppermute | solution.py:482
  96.5 27.6 %copy-start.4 = (bf16[2,768,256]{2,1,0:T(8,128)(2,1)S(1)}, bf16[2,768,256]{2,1,0:T(8,128)(2,1)}, u32[]{:S(2)}) copy-start(bf16[2,768,256]{2,1,0:T(8,128)(2,1)} %constant.46.clone.t_hbm) | copy-start | bytes 2359300
  124.1 9.2 %copy-start.2 = (f32[128,4,8,128]{3,2,1,0:T(8,128)S(1)}, f32[128,4,8,128]{3,2,1,0:T(8,128)}, u32[]{:S(2)}) copy-start(f32[128,4,8,128]{3,2,1,0:T(8,128)} %get-tuple-element.22.inv_hbm) | copy-start | bytes 6291460
  124.1 9.2 %copy-start.5 = (f32[128]{0:T(128)S(1)}, f32[128]{0:T(128)}, u32[]{:S(2)}) copy-start(f32[128]{0:T(128)} %get-tuple-element.29.up_ref) | copy-start | bytes 1540
  124.1 9.2 %copy-start.6 = (f32[128]{0:T(128)S(1)}, f32[128]{0:T(128)}, u32[]{:S(2)}) copy-start(f32[128]{0:T(128)} %get-tuple-element.30.low_ref) | copy-start | bytes 1540
  128.3 9.2 %collective-permute-start.7 = (f32[2,4,8,128]{3,2,1,0:T(8,128)S(1)}, f32[2,4,8,128]{3,2,1,0:T(8,128)S(1)}, u32[]{:S(2)}, u32[]{:S(2)}) collective-permute-start(f32[2,4,8,128]{3,2,1,0:T(8,128)S(1)} %get-tuple-element.23.refs_0_), channel_id=1, source_target_pairs={{0,3},{1,0},{2,1},{3,2},{4,7},{5,4},{6,5},{7,6},{8,11},{9,8},{10,9... | collective-permute-start | bytes 98312 | tf_op jit(solution)/shard_map/ppermute | solution.py:523
  128.8 8.7 %collective-permute-start.6 = (f32[2,4,8,128]{3,2,1,0:T(8,128)S(1)}, f32[2,4,8,128]{3,2,1,0:T(8,128)S(1)}, u32[]{:S(2)}, u32[]{:S(2)}) collective-permute-start(f32[2,4,8,128]{3,2,1,0:T(8,128)S(1)} %get-tuple-element.23.refs_0_), channel_id=1, source_target_pairs={{0,2},{1,3},{2,0},{3,1},{4,6},{5,7},{6,4},{7,5},{8,10},{9,11},{10,... | collective-permute-start | bytes 98312 | tf_op jit(solution)/shard_map/ppermute | solution.py:523
  131.4 6.1 %collective-permute-start.5 = (f32[2,4,8,128]{3,2,1,0:T(8,128)S(1)}, f32[2,4,8,128]{3,2,1,0:T(8,128)S(1)}, u32[]{:S(2)}, u32[]{:S(2)}) collective-permute-start(f32[2,4,8,128]{3,2,1,0:T(8,128)S(1)} %get-tuple-element.23.refs_0_), channel_id=1, source_target_pairs={{0,1},{1,2},{2,3},{3,0},{4,5},{5,6},{6,7},{7,4},{8,9},{9,10},{10,1... | collective-permute-start | bytes 98312 | tf_op jit(solution)/shard_map/ppermute | solution.py:523
  133.3 4.3 %copy-start = (f32[4,1024,128]{2,1,0:T(8,128)S(1)}, f32[4,1024,128]{2,1,0:T(8,128)}, u32[]{:S(2)}) copy-start(f32[4,1024,128]{2,1,0:T(8,128)} %get-tuple-element.19.v_hbm.refs_5_) | copy-start | bytes 6291460
  133.3 4.3 %copy-start.1 = (f32[4,1024,128]{2,1,0:T(8,128)S(1)}, f32[4,1024,128]{2,1,0:T(8,128)}, u32[]{:S(2)}) copy-start(f32[4,1024,128]{2,1,0:T(8,128)} %get-tuple-element.20.w_hbm.refs_6_) | copy-start | bytes 6291460
  133.3 4.3 %copy-start.3 = (bf16[2,256,768]{2,1,0:T(8,128)(2,1)S(1)}, bf16[2,256,768]{2,1,0:T(8,128)(2,1)}, u32[]{:S(2)}) copy-start(bf16[2,256,768]{2,1,0:T(8,128)(2,1)} %constant.47.clone.refs_7_.t_ref) | copy-start | bytes 2359300

commit v4 on v3

--- a/solution.py
+++ b/solution.py
@@ -179,19 +179,22 @@
         ends_ref[3, t] = w_ref[t, pl.ds(rows - 1, 8, stride=rows), :]
 
 
-def span_modes(x_ref, t_ref, mode):
+def span_sides(x_ref, mode, count):
     planes = x_ref.shape[0] // 8
-    both = [
-        jnp.transpose(x_ref[pl.ds(mode + p, planes, stride=8), :]) for p in range(2)
+    some = [
+        jnp.transpose(x_ref[pl.ds(mode + p, planes, stride=8), :]) for p in range(count)
     ]
-    x = jnp.concatenate(both, axis=0)
-    return jnp.concatenate([dot(part, t_ref[k]) for k, part in enumerate(folded(x, 1))], axis=1)
+    return folded(jnp.concatenate(some, axis=0), 1)
+
+
+def span_modes(sides, t_ref):
+    return jnp.concatenate([dot(part, t_ref[k]) for k, part in enumerate(sides)], axis=1)
 
 
 def span_first_kernel(x_ref, t_ref, o_ref):
     tiles = o_ref.shape[0]
     for mode in range(0, 8, 2):
-        y = span_modes(x_ref, t_ref, mode)
+        y = span_modes(span_sides(x_ref, mode, 2), t_ref)
         for t in range(tiles):
             o_ref[t, mode * 128 : (mode + 2) * 128, :] = y[:, t * 128 : (t + 1) * 128]
 
@@ -222,10 +225,14 @@
     for group in copies:
         for copy in group:
             copy.start()
-    table.wait()
     weight = weight_ref[...]
     for pair in range(4):
-        y = span_modes(x_ref, t, 2 * pair)
+        if pair % 2 == 0:
+            sides = span_sides(x_ref, 2 * pair, 4)
+            if pair == 0:
+                table.wait()
+            four = span_modes(sides, t)
+        y = four[pair % 2 * 256 : (pair % 2 + 1) * 256]
         for copy in copies[pair]:
             copy.wait()
         for p in range(2):

time: 199 us -> 199 us (level)
  no operation moved by 1% of the time
where the time goes in v4:
time: 199 us; the launch traced here: 198 us
  blocking collectives  56.5 us (28%)
  waiting for transfers between devices  55.9 us (28%)
  Pallas kernels  41.1 us (21%)
  starting transfers between devices  33.3 us (17%)
  local copies, waits for them, and re-layouts  7.06 us (4%)
  other arithmetic  4.07 us (2%)
    all_to_all x1, blocking collectives, moved(): return lax.all_to_all(x, both, split_axis=0, concat_axis=0, tiled=True)  56.5 us
    all_to_all x2, waiting for transfers between devices, moved(): return lax.all_to_all(x, both, split_axis=0, concat_axis=0, tiled=True)  54.4 us
    all_to_all x2, starting transfers between devices, moved(): return lax.all_to_all(x, both, split_axis=0, concat_axis=0, tiled=True)  17.5 us
    pallas_call x1, Pallas kernels, local(): pl.pallas_call(factor_kernel, in_specs=[smem, smem, vmem], out_specs=[vme...  13.3 us
    pallas_call x1, Pallas kernels, local(): pl.pallas_call(flow_field_kernel, grid=(planes // 2,), in_specs=[plane_bl...  7.13 us
    ppermute x3, starting transfers between devices, local(): ends = [y_ends] + [lax.ppermute(y_ends, 'gy', ring) for ring in rings]  5.01 us
    ppermute x3, starting transfers between devices, local(): lax.ppermute(vw_ends, 'gy', ring)  4.93 us
    pallas_call x1, Pallas kernels, local(): pl.pallas_call(span_first_kernel, in_specs=[vmem, vmem], out_specs=vmem,...  4.39 us
  transfers between devices with their start and end apart: 10, of which 4 were waited for; matrix products, arithmetic and copies ran while one was open for 4% of the time, Pallas kernels for 15%

profile of v4, /device:TPU:8, one launch (start us, length us, event | category | flops | bytes accessed | tf_op | source)
XLA Modules:
  0.0 198.2 jit_solution(11600518023560910426)
XLA Ops:
  0.0 4.0 %span_field.1 = f32[64,8,8,128]{3,2,1,0:T(8,128)} custom-call(f32[3,8,512,128]{3,2,1,0:T(8,128)} %w_hbm.1, bf16[2,256,768]{2,1,0:T(8,128)(2,1)} %constant.41.clone.t_hbm), custom_call_target="tpu_custom_call" | custom-call | flops 1610612736 | bytes 4194304 | tf_op jit(solution)/shard_map/span_field/pallas_call | solution.py:422
  4.0 12.2 %all-to-all-start.1 = ((f32[64,8,8,128]{3,2,1,0:T(8,128)}), f32[64,8,8,128]{3,2,1,0:T(8,128)}, u32[]{:S(2)}, u32[]{:S(2)}) async-start(f32[64,8,8,128]{3,2,1,0:T(8,128)} %span_field.1), calls=%async_computation.1 | async-start | bytes 4194304 | tf_op jit(solution)/shard_map/all_to_all | solution.py:414
  16.2 1.6 slice-done
  17.8 2.0 copy.12
  19.8 0.7 slice_bitcast_fusion
  20.5 2.4 %collective-permute-start.1 = (f32[8,512]{1,0:T(8,128)S(1)}, f32[8,512]{1,0:T(8,128)S(1)}, u32[]{:S(2)}, u32[]{:S(2)}) collective-permute-start(f32[8,512]{1,0:T(8,128)S(1)} %get-tuple-element.27), channel_id=1, source_target_pairs={{1,0},{2,1},{3,2},{5,4},{6,5},{7,6},{9,8},{10,9},{11,10},{13,12},{... | collective-permute-start | bytes 49160 | tf_op jit(solution)/shard_map/ppermute | solution.py:443
  22.9 3.5 %collective-permute-start = (f32[8,512]{1,0:T(8,128)S(1)}, f32[8,512]{1,0:T(8,128)S(1)}, u32[]{:S(2)}, u32[]{:S(2)}) collective-permute-start(f32[8,512]{1,0:T(8,128)S(1)} %get-tuple-element.28), channel_id=1, source_target_pairs={{0,1},{1,2},{2,3},{4,5},{5,6},{6,7},{8,9},{9,10},{10,11},{12,13},{... | collective-permute-start | bytes 49160 | tf_op jit(solution)/shard_map/ppermute | solution.py:442
  26.3 0.8 dynamic_slice.6
  27.1 0.7 broadcast_multiply_fusion
  27.8 0.7 collective-permute-done.before_ref
  28.5 0.6 copy-done.8
  29.1 7.1 %flow_field.1 = f32[64,8,8,128]{3,2,1,0:T(8,128)} custom-call(f32[3,8,512,128]{3,2,1,0:T(8,128)} %w_hbm.1, f32[3,8,512,128]{3,2,1,0:T(8,128)} %w_hbm.1, f32[8,512]{1,0:T(8,128)} %copy-done.8, f32[8,512]{1,0:T(8,128)} %copy-done.7, f32[1,128]{1,0:T(1,128)} %bitcast.21, bf16[2,256,1536]{2,1,0:T(8,128)(2,1)} %constant.42.clone.t_ref), custom_call_target="tpu_custom_call" | custom-call | flops 3221225472 | bytes 6291456 | tf_op jit(solution)/shard_map/flow_field/pallas_call | solution.py:451
  36.2 31.2 %all-to-all-done.1 = f32[64,8,8,128]{3,2,1,0:T(8,128)} async-done(((f32[64,8,8,128]{3,2,1,0:T(8,128)}), f32[64,8,8,128]{3,2,1,0:T(8,128)}, u32[]{:S(2)}, u32[]{:S(2)}) %all-to-all-start.1) | async-done | bytes 2097184 | tf_op jit(solution)/shard_map/all_to_all | solution.py:414
  67.4 5.3 %all-to-all-start = ((f32[64,8,8,128]{3,2,1,0:T(8,128)}), f32[64,8,8,128]{3,2,1,0:T(8,128)S(1)}, u32[]{:S(2)}, u32[]{:S(2)}) async-start(f32[64,8,8,128]{3,2,1,0:T(8,128)} %flow_field.1), calls=%async_computation | async-start | bytes 4194304 | tf_op jit(solution)/shard_map/all_to_all | solution.py:414
  72.7 0.8 dynamic_slice.7
  73.5 0.6 multiply_divide_fusion
  74.1 0.7 broadcast_add_fusion.sigma_ref
  74.7 13.3 %factor.1 = (f32[128,4,8,128]{3,2,1,0:T(8,128)}, f32[4,1024,128]{2,1,0:T(8,128)}, f32[4,1024,128]{2,1,0:T(8,128)}, f32[4,4,8,128]{3,2,1,0:T(8,128)}) custom-call(f32[128]{0:T(128)} %get-tuple-element.30.low_ref, f32[128]{0:T(128)} %get-tuple-element.29.up_ref, f32[4,8,128]{2,1,0:T(8,128)} %broadcast_add_fusion.sigma_ref), custom_call_target="tpu_custom_call" | custom-call | flops 1610612736 | bytes 6291456 | tf_op jit(solution)/shard_map/factor/pallas_call | solution.py:477
  88.5 2.6 %collective-permute-start.3 = (f32[4,4,8,128]{3,2,1,0:T(8,128)}, f32[4,4,8,128]{3,2,1,0:T(8,128)S(1)}, u32[]{:S(2)}, u32[]{:S(2)}) collective-permute-start(f32[4,4,8,128]{3,2,1,0:T(8,128)} %get-tuple-element.15), channel_id=1, source_target_pairs={{0,2},{1,3},{2,0},{3,1},{4,6},{5,7},{6,4},{7,5},{8,10},{9,11},{10,... | collective-permute-start | bytes 196616 | tf_op jit(solution)/shard_map/ppermute | solution.py:489
  91.0 1.9 collective-permute-start.2
  93.5 1.3 pad_maximum_fusion.1.gap_ref
  94.8 0.7 collective-permute-done.2
  95.5 0.9 pad_maximum_fusion.refs_4_
  96.5 4.4 %span_first.1.s_hbm = f32[4,1024,128]{2,1,0:T(8,128)} custom-call(f32[4096,128]{1,0:T(8,128)} %bitcast.10.x_ref, bf16[2,768,256]{2,1,0:T(8,128)(2,1)} %constant.45.clone.t_ref), custom_call_target="tpu_custom_call" | custom-call | flops 1610612736 | bytes 4194304 | tf_op jit(solution)/shard_map/span_first/pallas_call | solution.py:496
  100.9 23.2 %all-to-all-done = f32[64,8,8,128]{3,2,1,0:T(8,128)S(1)} async-done(((f32[64,8,8,128]{3,2,1,0:T(8,128)}), f32[64,8,8,128]{3,2,1,0:T(8,128)S(1)}, u32[]{:S(2)}, u32[]{:S(2)}) %all-to-all-start) | async-done | bytes 2097184 | tf_op jit(solution)/shard_map/all_to_all | solution.py:414
  124.1 3.9 %source.1 = (f32[4,1024,128]{2,1,0:T(8,128)S(1)}, f32[2,4,8,128]{3,2,1,0:T(8,128)S(1)}) custom-call(f32[4096,128]{1,0:T(8,128)S(1)} %bitcast.14, f32[128,128]{1,0:T(8,128)S(1)} %broadcast_in_dim.2.weight_ref, f32[2]{0:T(128)S(1)} %pad_maximum_fusion.1.gap_ref, bf16[2,768,256]{2,1,0:T(8,128)(2,1)S(1)} %copy-done.4, f32[4,1024,128]{2,1,0:T(8,128)} %span_first.1.s_hbm, ...), custom_call_target="tpu_custom_call" | custom-call | flops 1610612736 | bytes 10485760 | tf_op jit(solution)/shard_map/source/pallas_call | solution.py:506
  128.6 2.6 %collective-permute-start.6 = (f32[2,4,8,128]{3,2,1,0:T(8,128)S(1)}, f32[2,4,8,128]{3,2,1,0:T(8,128)S(1)}, u32[]{:S(2)}, u32[]{:S(2)}) collective-permute-start(f32[2,4,8,128]{3,2,1,0:T(8,128)S(1)} %get-tuple-element.23.refs_0_), channel_id=1, source_target_pairs={{0,2},{1,3},{2,0},{3,1},{4,6},{5,7},{6,4},{7,5},{8,10},{9,11},{10,... | collective-permute-start | bytes 98312 | tf_op jit(solution)/shard_map/ppermute | solution.py:530
  131.1 1.9 collective-permute-start.5
  133.1 4.2 %sweep.1.y_ref = f32[4,1024,128]{2,1,0:T(8,128)S(1)} custom-call(f32[128]{0:T(128)S(1)} %copy-done.6, f32[128]{0:T(128)S(1)} %copy-done.5, f32[4,1024,128]{2,1,0:T(8,128)S(1)} %get-tuple-element.21.x_ref, f32[128,4,8,128]{3,2,1,0:T(8,128)S(1)} %copy-done.2), custom_call_target="tpu_custom_call" | custom-call | flops 1610612736 | bytes 6291456 | tf_op jit(solution)/shard_map/sweep/pallas_call | solution.py:532
  137.3 2.2 %join.1 = f32[64,8,8,128]{3,2,1,0:T(8,128)S(1)} custom-call(s32[1]{0:T(128)} %bitcast.me_ref, f32[4,1024,128]{2,1,0:T(8,128)S(1)} %sweep.1.y_ref, f32[2,4,8,128]{3,2,1,0:T(8,128)S(1)} %get-tuple-element.23.refs_0_, f32[2,4,8,128]{3,2,1,0:T(8,128)S(1)} %collective-permute-done.5.refs_1_, f32[2,4,8,128]{3,2,1,0:T(8,128)S(1)} %collective-permute-done.6.refs_2_, ...), custom_call_target="tpu_custom_call" | custom-call | flops 1610612736 | bytes 8388608 | tf_op jit(solution)/shard_map/join/pallas_call | solution.py:543
  139.6 56.5 %all_to_all.15 = f32[64,8,8,128]{3,2,1,0:T(8,128)S(1)} all-to-all(f32[64,8,8,128]{3,2,1,0:T(8,128)S(1)} %join.1), channel_id=1, replica_groups=mesh['gx'=8,'gz'=8,'gy'=4] {'gx','gz'}, dimensions={0} | all-to-all | bytes 4194304 | tf_op jit(solution)/shard_map/all_to_all | solution.py:414
  196.1 2.0 %flow_inverse.1 = f32[8,512,128]{2,1,0:T(8,128)} custom-call(f32[4096,128]{1,0:T(8,128)S(1)} %bitcast.15, bf16[2,256,768]{2,1,0:T(8,128)(2,1)S(1)} %copy-done.3), custom_call_target="tpu_custom_call" | custom-call | flops 1610612736 | bytes 4194304 | tf_op jit(solution)/shard_map/flow_inverse/pallas_call | solution.py:571
  (32 shorter events, 1.7 us)
Async XLA Ops:
  4.0 63.4 %all-to-all-start.1 = ((f32[64,8,8,128]{3,2,1,0:T(8,128)}), f32[64,8,8,128]{3,2,1,0:T(8,128)}, u32[]{:S(2)}, u32[]{:S(2)}) async-start(f32[64,8,8,128]{3,2,1,0:T(8,128)} %span_field.1), calls=%async_computation.1 | async-start | bytes 4194304 | tf_op jit(solution)/shard_map/all_to_all | solution.py:414
  16.2 1.6 slice-start
  20.5 7.3 %collective-permute-start.1 = (f32[8,512]{1,0:T(8,128)S(1)}, f32[8,512]{1,0:T(8,128)S(1)}, u32[]{:S(2)}, u32[]{:S(2)}) collective-permute-start(f32[8,512]{1,0:T(8,128)S(1)} %get-tuple-element.27), channel_id=1, source_target_pairs={{1,0},{2,1},{3,2},{5,4},{6,5},{7,6},{9,8},{10,9},{11,10},{13,12},{... | collective-permute-start | bytes 49160 | tf_op jit(solution)/shard_map/ppermute | solution.py:443
  22.9 5.6 %collective-permute-start = (f32[8,512]{1,0:T(8,128)S(1)}, f32[8,512]{1,0:T(8,128)S(1)}, u32[]{:S(2)}, u32[]{:S(2)}) collective-permute-start(f32[8,512]{1,0:T(8,128)S(1)} %get-tuple-element.28), channel_id=1, source_target_pairs={{0,1},{1,2},{2,3},{4,5},{5,6},{6,7},{8,9},{9,10},{10,11},{12,13},{... | collective-permute-start | bytes 49160 | tf_op jit(solution)/shard_map/ppermute | solution.py:442
  27.8 0.7 copy-start.7
  28.5 0.6 copy-start.8
  36.2 37.3 %copy-start.9 = (f32[128]{0:T(128)S(1)}, f32[128]{0:T(128)}, u32[]{:S(2)}) copy-start(f32[128]{0:T(128)} %get-tuple-element.26) | copy-start | bytes 1540
  36.2 37.9 %copy-start.10 = (f32[4,128]{1,0:T(4,128)S(1)}, f32[4,128]{1,0:T(4,128)}, u32[]{:S(2)}) copy-start(f32[4,128]{1,0:T(4,128)} %constant.49) | copy-start | bytes 6148
  67.4 56.7 %all-to-all-start = ((f32[64,8,8,128]{3,2,1,0:T(8,128)}), f32[64,8,8,128]{3,2,1,0:T(8,128)S(1)}, u32[]{:S(2)}, u32[]{:S(2)}) async-start(f32[64,8,8,128]{3,2,1,0:T(8,128)} %flow_field.1), calls=%async_computation | async-start | bytes 4194304 | tf_op jit(solution)/shard_map/all_to_all | solution.py:414
  88.0 6.8 %collective-permute-start.4 = (f32[4,4,8,128]{3,2,1,0:T(8,128)}, f32[4,4,8,128]{3,2,1,0:T(8,128)S(1)}, u32[]{:S(2)}, u32[]{:S(2)}) collective-permute-start(f32[4,4,8,128]{3,2,1,0:T(8,128)} %get-tuple-element.15), channel_id=1, source_target_pairs={{0,3},{1,0},{2,1},{3,2},{4,7},{5,4},{6,5},{7,6},{8,11},{9,8},{10,9... | collective-permute-start | bytes 196616 | tf_op jit(solution)/shard_map/ppermute | solution.py:489
  88.5 6.4 %collective-permute-start.3 = (f32[4,4,8,128]{3,2,1,0:T(8,128)}, f32[4,4,8,128]{3,2,1,0:T(8,128)S(1)}, u32[]{:S(2)}, u32[]{:S(2)}) collective-permute-start(f32[4,4,8,128]{3,2,1,0:T(8,128)} %get-tuple-element.15), channel_id=1, source_target_pairs={{0,2},{1,3},{2,0},{3,1},{4,6},{5,7},{6,4},{7,5},{8,10},{9,11},{10,... | collective-permute-start | bytes 196616 | tf_op jit(solution)/shard_map/ppermute | solution.py:489
  91.0 4.5 %collective-permute-start.2 = (f32[4,4,8,128]{3,2,1,0:T(8,128)}, f32[4,4,8,128]{3,2,1,0:T(8,128)S(1)}, u32[]{:S(2)}, u32[]{:S(2)}) collective-permute-start(f32[4,4,8,128]{3,2,1,0:T(8,128)} %get-tuple-element.15), channel_id=1, source_target_pairs={{0,1},{1,2},{2,3},{3,0},{4,5},{5,6},{6,7},{7,4},{8,9},{9,10},{10,1... | collective-permute-start | bytes 196616 | tf_op jit(solution)/shard_map/ppermute | solution.py:489
  96.5 27.6 %copy-start.4 = (bf16[2,768,256]{2,1,0:T(8,128)(2,1)S(1)}, bf16[2,768,256]{2,1,0:T(8,128)(2,1)}, u32[]{:S(2)}) copy-start(bf16[2,768,256]{2,1,0:T(8,128)(2,1)} %constant.46.clone.t_hbm) | copy-start | bytes 2359300
  124.1 8.9 %copy-start.2 = (f32[128,4,8,128]{3,2,1,0:T(8,128)S(1)}, f32[128,4,8,128]{3,2,1,0:T(8,128)}, u32[]{:S(2)}) copy-start(f32[128,4,8,128]{3,2,1,0:T(8,128)} %get-tuple-element.22.inv_hbm) | copy-start | bytes 6291460
  124.1 8.9 %copy-start.5 = (f32[128]{0:T(128)S(1)}, f32[128]{0:T(128)}, u32[]{:S(2)}) copy-start(f32[128]{0:T(128)} %get-tuple-element.29.up_ref) | copy-start | bytes 1540
  124.1 8.9 %copy-start.6 = (f32[128]{0:T(128)S(1)}, f32[128]{0:T(128)}, u32[]{:S(2)}) copy-start(f32[128]{0:T(128)} %get-tuple-element.30.low_ref) | copy-start | bytes 1540
  128.0 9.2 %collective-permute-start.7 = (f32[2,4,8,128]{3,2,1,0:T(8,128)S(1)}, f32[2,4,8,128]{3,2,1,0:T(8,128)S(1)}, u32[]{:S(2)}, u32[]{:S(2)}) collective-permute-start(f32[2,4,8,128]{3,2,1,0:T(8,128)S(1)} %get-tuple-element.23.refs_0_), channel_id=1, source_target_pairs={{0,3},{1,0},{2,1},{3,2},{4,7},{5,4},{6,5},{7,6},{8,11},{9,8},{10,9... | collective-permute-start | bytes 98312 | tf_op jit(solution)/shard_map/ppermute | solution.py:530
  128.6 8.7 %collective-permute-start.6 = (f32[2,4,8,128]{3,2,1,0:T(8,128)S(1)}, f32[2,4,8,128]{3,2,1,0:T(8,128)S(1)}, u32[]{:S(2)}, u32[]{:S(2)}) collective-permute-start(f32[2,4,8,128]{3,2,1,0:T(8,128)S(1)} %get-tuple-element.23.refs_0_), channel_id=1, source_target_pairs={{0,2},{1,3},{2,0},{3,1},{4,6},{5,7},{6,4},{7,5},{8,10},{9,11},{10,... | collective-permute-start | bytes 98312 | tf_op jit(solution)/shard_map/ppermute | solution.py:530
  131.1 6.1 %collective-permute-start.5 = (f32[2,4,8,128]{3,2,1,0:T(8,128)S(1)}, f32[2,4,8,128]{3,2,1,0:T(8,128)S(1)}, u32[]{:S(2)}, u32[]{:S(2)}) collective-permute-start(f32[2,4,8,128]{3,2,1,0:T(8,128)S(1)} %get-tuple-element.23.refs_0_), channel_id=1, source_target_pairs={{0,1},{1,2},{2,3},{3,0},{4,5},{5,6},{6,7},{7,4},{8,9},{9,10},{10,1... | collective-permute-start | bytes 98312 | tf_op jit(solution)/shard_map/ppermute | solution.py:530
  133.0 4.3 %copy-start = (f32[4,1024,128]{2,1,0:T(8,128)S(1)}, f32[4,1024,128]{2,1,0:T(8,128)}, u32[]{:S(2)}) copy-start(f32[4,1024,128]{2,1,0:T(8,128)} %get-tuple-element.19.v_hbm.refs_5_) | copy-start | bytes 6291460
  133.0 4.3 %copy-start.1 = (f32[4,1024,128]{2,1,0:T(8,128)S(1)}, f32[4,1024,128]{2,1,0:T(8,128)}, u32[]{:S(2)}) copy-start(f32[4,1024,128]{2,1,0:T(8,128)} %get-tuple-element.20.w_hbm.refs_6_) | copy-start | bytes 6291460
  133.1 4.3 %copy-start.3 = (bf16[2,256,768]{2,1,0:T(8,128)(2,1)S(1)}, bf16[2,256,768]{2,1,0:T(8,128)(2,1)}, u32[]{:S(2)}) copy-start(bf16[2,256,768]{2,1,0:T(8,128)(2,1)} %constant.47.clone.refs_7_.t_ref) | copy-start | bytes 2359300

commit v5 on v4

--- a/solution.py
+++ b/solution.py
@@ -343,16 +343,14 @@
             b_ref[g + 1, tile] = alphas[g] + betas[g] * after
             after = starts[g] + scales[g] * after
             f_ref[g, tile] = after
-    for pair in range(4):
-        for copy in copies[pair]:
+    for quad in range(2):
+        for copy in copies[2 * quad] + copies[2 * quad + 1]:
             copy.wait()
-        if pair == 0:
-            table.wait()
         columns = []
         for tile in range(tiles):
             both = []
-            for p in range(2):
-                mode = 2 * pair + p
+            for p in range(4):
+                mode = 4 * quad + p
                 part = slice(mode * 128, (mode + 1) * 128)
                 left = b_ref[me, tile, pl.ds(mode, 1), :]
                 right = f_ref[me + 1, tile, pl.ds(mode, 1), :]
@@ -360,6 +358,8 @@
                     y_ref[tile, part, :] + v[tile, part, :] * left + w[tile, part, :] * right
                 )
             columns.append(jnp.concatenate(both, axis=0))
+        if quad == 0:
+            table.wait()
         half = tiles // 2
         y = to_nodes(
             *(
@@ -372,9 +372,9 @@
                 for k in range(2)
             )
         )
-        for p in range(2):
+        for p in range(4):
             part = y[:, 128 * p : 128 * (p + 1)]
-            o_ref[:, 2 * pair + p] = part.reshape(part.shape[0] // 8, 8, 128)
+            o_ref[:, 4 * quad + p] = part.reshape(part.shape[0] // 8, 8, 128)
 
 
 def flow_inverse_kernel(x_ref, t_ref, o_hbm, o, sems):

time: 199 us -> 199 us (level)
  no operation moved by 1% of the time
where the time goes in v5:
time: 199 us; the launch traced here: 198 us
  blocking collectives  56.5 us (28%)
  waiting for transfers between devices  55.9 us (28%)
  Pallas kernels  40.8 us (21%)
  starting transfers between devices  33.3 us (17%)
  local copies, waits for them, and re-layouts  7.06 us (4%)
  other arithmetic  4.07 us (2%)
    all_to_all x1, blocking collectives, moved(): return lax.all_to_all(x, both, split_axis=0, concat_axis=0, tiled=True)  56.5 us
    all_to_all x2, waiting for transfers between devices, moved(): return lax.all_to_all(x, both, split_axis=0, concat_axis=0, tiled=True)  54.4 us
    all_to_all x2, starting transfers between devices, moved(): return lax.all_to_all(x, both, split_axis=0, concat_axis=0, tiled=True)  17.5 us
    pallas_call x1, Pallas kernels, local(): pl.pallas_call(factor_kernel, in_specs=[smem, smem, vmem], out_specs=[vme...  13.3 us
    pallas_call x1, Pallas kernels, local(): pl.pallas_call(flow_field_kernel, grid=(planes // 2,), in_specs=[plane_bl...  7.13 us
    ppermute x3, starting transfers between devices, local(): ends = [y_ends] + [lax.ppermute(y_ends, 'gy', ring) for ring in rings]  5.01 us
    ppermute x3, starting transfers between devices, local(): lax.ppermute(vw_ends, 'gy', ring)  4.93 us
    pallas_call x1, Pallas kernels, local(): pl.pallas_call(span_first_kernel, in_specs=[vmem, vmem], out_specs=vmem,...  4.39 us
  transfers between devices with their start and end apart: 10, of which 4 were waited for; matrix products, arithmetic and copies ran while one was open for 4% of the time, Pallas kernels for 15%

profile of v5, /device:TPU:8, one launch (start us, length us, event | category | flops | bytes accessed | tf_op | source)
XLA Modules:
  0.0 197.9 jit_solution(17112886214452366892)
XLA Ops:
  0.0 4.0 %span_field.1 = f32[64,8,8,128]{3,2,1,0:T(8,128)} custom-call(f32[3,8,512,128]{3,2,1,0:T(8,128)} %w_hbm.1, bf16[2,256,768]{2,1,0:T(8,128)(2,1)} %constant.41.clone.t_hbm), custom_call_target="tpu_custom_call" | custom-call | flops 1610612736 | bytes 4194304 | tf_op jit(solution)/shard_map/span_field/pallas_call | solution.py:422
  4.0 12.2 %all-to-all-start.1 = ((f32[64,8,8,128]{3,2,1,0:T(8,128)}), f32[64,8,8,128]{3,2,1,0:T(8,128)}, u32[]{:S(2)}, u32[]{:S(2)}) async-start(f32[64,8,8,128]{3,2,1,0:T(8,128)} %span_field.1), calls=%async_computation.1 | async-start | bytes 4194304 | tf_op jit(solution)/shard_map/all_to_all | solution.py:414
  16.2 1.6 slice-done
  17.8 2.0 copy.12
  19.8 0.7 slice_bitcast_fusion
  20.5 2.4 %collective-permute-start.1 = (f32[8,512]{1,0:T(8,128)S(1)}, f32[8,512]{1,0:T(8,128)S(1)}, u32[]{:S(2)}, u32[]{:S(2)}) collective-permute-start(f32[8,512]{1,0:T(8,128)S(1)} %get-tuple-element.27), channel_id=1, source_target_pairs={{1,0},{2,1},{3,2},{5,4},{6,5},{7,6},{9,8},{10,9},{11,10},{13,12},{... | collective-permute-start | bytes 49160 | tf_op jit(solution)/shard_map/ppermute | solution.py:443
  22.9 3.5 %collective-permute-start = (f32[8,512]{1,0:T(8,128)S(1)}, f32[8,512]{1,0:T(8,128)S(1)}, u32[]{:S(2)}, u32[]{:S(2)}) collective-permute-start(f32[8,512]{1,0:T(8,128)S(1)} %get-tuple-element.28), channel_id=1, source_target_pairs={{0,1},{1,2},{2,3},{4,5},{5,6},{6,7},{8,9},{9,10},{10,11},{12,13},{... | collective-permute-start | bytes 49160 | tf_op jit(solution)/shard_map/ppermute | solution.py:442
  26.3 0.8 dynamic_slice.6
  27.1 0.7 broadcast_multiply_fusion
  27.8 0.7 collective-permute-done.before_ref
  28.5 0.6 copy-done.8
  29.1 7.1 %flow_field.1 = f32[64,8,8,128]{3,2,1,0:T(8,128)} custom-call(f32[3,8,512,128]{3,2,1,0:T(8,128)} %w_hbm.1, f32[3,8,512,128]{3,2,1,0:T(8,128)} %w_hbm.1, f32[8,512]{1,0:T(8,128)} %copy-done.8, f32[8,512]{1,0:T(8,128)} %copy-done.7, f32[1,128]{1,0:T(1,128)} %bitcast.21, bf16[2,256,1536]{2,1,0:T(8,128)(2,1)} %constant.42.clone.t_ref), custom_call_target="tpu_custom_call" | custom-call | flops 3221225472 | bytes 6291456 | tf_op jit(solution)/shard_map/flow_field/pallas_call | solution.py:451
  36.2 31.2 %all-to-all-done.1 = f32[64,8,8,128]{3,2,1,0:T(8,128)} async-done(((f32[64,8,8,128]{3,2,1,0:T(8,128)}), f32[64,8,8,128]{3,2,1,0:T(8,128)}, u32[]{:S(2)}, u32[]{:S(2)}) %all-to-all-start.1) | async-done | bytes 2097184 | tf_op jit(solution)/shard_map/all_to_all | solution.py:414
  67.4 5.3 %all-to-all-start = ((f32[64,8,8,128]{3,2,1,0:T(8,128)}), f32[64,8,8,128]{3,2,1,0:T(8,128)S(1)}, u32[]{:S(2)}, u32[]{:S(2)}) async-start(f32[64,8,8,128]{3,2,1,0:T(8,128)} %flow_field.1), calls=%async_computation | async-start | bytes 4194304 | tf_op jit(solution)/shard_map/all_to_all | solution.py:414
  72.7 0.8 dynamic_slice.7
  73.5 0.6 multiply_divide_fusion
  74.1 0.7 broadcast_add_fusion.sigma_ref
  74.7 13.3 %factor.1 = (f32[128,4,8,128]{3,2,1,0:T(8,128)}, f32[4,1024,128]{2,1,0:T(8,128)}, f32[4,1024,128]{2,1,0:T(8,128)}, f32[4,4,8,128]{3,2,1,0:T(8,128)}) custom-call(f32[128]{0:T(128)} %get-tuple-element.30.low_ref, f32[128]{0:T(128)} %get-tuple-element.29.up_ref, f32[4,8,128]{2,1,0:T(8,128)} %broadcast_add_fusion.sigma_ref), custom_call_target="tpu_custom_call" | custom-call | flops 1610612736 | bytes 6291456 | tf_op jit(solution)/shard_map/factor/pallas_call | solution.py:477
  88.5 2.6 %collective-permute-start.3 = (f32[4,4,8,128]{3,2,1,0:T(8,128)}, f32[4,4,8,128]{3,2,1,0:T(8,128)S(1)}, u32[]{:S(2)}, u32[]{:S(2)}) collective-permute-start(f32[4,4,8,128]{3,2,1,0:T(8,128)} %get-tuple-element.15), channel_id=1, source_target_pairs={{0,2},{1,3},{2,0},{3,1},{4,6},{5,7},{6,4},{7,5},{8,10},{9,11},{10,... | collective-permute-start | bytes 196616 | tf_op jit(solution)/shard_map/ppermute | solution.py:489
  91.0 1.9 collective-permute-start.2
  93.5 1.3 pad_maximum_fusion.1.gap_ref
  94.8 0.7 collective-permute-done.2
  95.5 0.9 pad_maximum_fusion.refs_4_
  96.5 4.4 %span_first.1.s_hbm = f32[4,1024,128]{2,1,0:T(8,128)} custom-call(f32[4096,128]{1,0:T(8,128)} %bitcast.10.x_ref, bf16[2,768,256]{2,1,0:T(8,128)(2,1)} %constant.45.clone.t_ref), custom_call_target="tpu_custom_call" | custom-call | flops 1610612736 | bytes 4194304 | tf_op jit(solution)/shard_map/span_first/pallas_call | solution.py:496
  100.9 23.2 %all-to-all-done = f32[64,8,8,128]{3,2,1,0:T(8,128)S(1)} async-done(((f32[64,8,8,128]{3,2,1,0:T(8,128)}), f32[64,8,8,128]{3,2,1,0:T(8,128)S(1)}, u32[]{:S(2)}, u32[]{:S(2)}) %all-to-all-start) | async-done | bytes 2097184 | tf_op jit(solution)/shard_map/all_to_all | solution.py:414
  124.1 3.9 %source.1 = (f32[4,1024,128]{2,1,0:T(8,128)S(1)}, f32[2,4,8,128]{3,2,1,0:T(8,128)S(1)}) custom-call(f32[4096,128]{1,0:T(8,128)S(1)} %bitcast.14, f32[128,128]{1,0:T(8,128)S(1)} %broadcast_in_dim.2.weight_ref, f32[2]{0:T(128)S(1)} %pad_maximum_fusion.1.gap_ref, bf16[2,768,256]{2,1,0:T(8,128)(2,1)S(1)} %copy-done.4, f32[4,1024,128]{2,1,0:T(8,128)} %span_first.1.s_hbm, ...), custom_call_target="tpu_custom_call" | custom-call | flops 1610612736 | bytes 10485760 | tf_op jit(solution)/shard_map/source/pallas_call | solution.py:506
  128.6 2.6 %collective-permute-start.6 = (f32[2,4,8,128]{3,2,1,0:T(8,128)S(1)}, f32[2,4,8,128]{3,2,1,0:T(8,128)S(1)}, u32[]{:S(2)}, u32[]{:S(2)}) collective-permute-start(f32[2,4,8,128]{3,2,1,0:T(8,128)S(1)} %get-tuple-element.23.refs_0_), channel_id=1, source_target_pairs={{0,2},{1,3},{2,0},{3,1},{4,6},{5,7},{6,4},{7,5},{8,10},{9,11},{10,... | collective-permute-start | bytes 98312 | tf_op jit(solution)/shard_map/ppermute | solution.py:530
  131.1 1.9 collective-permute-start.5
  133.1 4.2 %sweep.1.y_ref = f32[4,1024,128]{2,1,0:T(8,128)S(1)} custom-call(f32[128]{0:T(128)S(1)} %copy-done.6, f32[128]{0:T(128)S(1)} %copy-done.5, f32[4,1024,128]{2,1,0:T(8,128)S(1)} %get-tuple-element.21.x_ref, f32[128,4,8,128]{3,2,1,0:T(8,128)S(1)} %copy-done.2), custom_call_target="tpu_custom_call" | custom-call | flops 1610612736 | bytes 6291456 | tf_op jit(solution)/shard_map/sweep/pallas_call | solution.py:532
  137.3 1.9 join.1
  139.3 56.5 %all_to_all.15 = f32[64,8,8,128]{3,2,1,0:T(8,128)S(1)} all-to-all(f32[64,8,8,128]{3,2,1,0:T(8,128)S(1)} %join.1), channel_id=1, replica_groups=mesh['gx'=8,'gz'=8,'gy'=4] {'gx','gz'}, dimensions={0} | all-to-all | bytes 4194304 | tf_op jit(solution)/shard_map/all_to_all | solution.py:414
  195.8 2.0 %flow_inverse.1 = f32[8,512,128]{2,1,0:T(8,128)} custom-call(f32[4096,128]{1,0:T(8,128)S(1)} %bitcast.15, bf16[2,256,768]{2,1,0:T(8,128)(2,1)S(1)} %copy-done.3), custom_call_target="tpu_custom_call" | custom-call | flops 1610612736 | bytes 4194304 | tf_op jit(solution)/shard_map/flow_inverse/pallas_call | solution.py:571
  (32 shorter events, 1.7 us)
Async XLA Ops:
  4.0 63.4 %all-to-all-start.1 = ((f32[64,8,8,128]{3,2,1,0:T(8,128)}), f32[64,8,8,128]{3,2,1,0:T(8,128)}, u32[]{:S(2)}, u32[]{:S(2)}) async-start(f32[64,8,8,128]{3,2,1,0:T(8,128)} %span_field.1), calls=%async_computation.1 | async-start | bytes 4194304 | tf_op jit(solution)/shard_map/all_to_all | solution.py:414
  16.2 1.6 slice-start
  20.5 7.3 %collective-permute-start.1 = (f32[8,512]{1,0:T(8,128)S(1)}, f32[8,512]{1,0:T(8,128)S(1)}, u32[]{:S(2)}, u32[]{:S(2)}) collective-permute-start(f32[8,512]{1,0:T(8,128)S(1)} %get-tuple-element.27), channel_id=1, source_target_pairs={{1,0},{2,1},{3,2},{5,4},{6,5},{7,6},{9,8},{10,9},{11,10},{13,12},{... | collective-permute-start | bytes 49160 | tf_op jit(solution)/shard_map/ppermute | solution.py:443
  22.9 5.6 %collective-permute-start = (f32[8,512]{1,0:T(8,128)S(1)}, f32[8,512]{1,0:T(8,128)S(1)}, u32[]{:S(2)}, u32[]{:S(2)}) collective-permute-start(f32[8,512]{1,0:T(8,128)S(1)} %get-tuple-element.28), channel_id=1, source_target_pairs={{0,1},{1,2},{2,3},{4,5},{5,6},{6,7},{8,9},{9,10},{10,11},{12,13},{... | collective-permute-start | bytes 49160 | tf_op jit(solution)/shard_map/ppermute | solution.py:442
  27.8 0.7 copy-start.7
  28.5 0.6 copy-start.8
  36.2 37.3 %copy-start.9 = (f32[128]{0:T(128)S(1)}, f32[128]{0:T(128)}, u32[]{:S(2)}) copy-start(f32[128]{0:T(128)} %get-tuple-element.26) | copy-start | bytes 1540
  36.2 37.9 %copy-start.10 = (f32[4,128]{1,0:T(4,128)S(1)}, f32[4,128]{1,0:T(4,128)}, u32[]{:S(2)}) copy-start(f32[4,128]{1,0:T(4,128)} %constant.49) | copy-start | bytes 6148
  67.4 56.7 %all-to-all-start = ((f32[64,8,8,128]{3,2,1,0:T(8,128)}), f32[64,8,8,128]{3,2,1,0:T(8,128)S(1)}, u32[]{:S(2)}, u32[]{:S(2)}) async-start(f32[64,8,8,128]{3,2,1,0:T(8,128)} %flow_field.1), calls=%async_computation | async-start | bytes 4194304 | tf_op jit(solution)/shard_map/all_to_all | solution.py:414
  88.0 6.8 %collective-permute-start.4 = (f32[4,4,8,128]{3,2,1,0:T(8,128)}, f32[4,4,8,128]{3,2,1,0:T(8,128)S(1)}, u32[]{:S(2)}, u32[]{:S(2)}) collective-permute-start(f32[4,4,8,128]{3,2,1,0:T(8,128)} %get-tuple-element.15), channel_id=1, source_target_pairs={{0,3},{1,0},{2,1},{3,2},{4,7},{5,4},{6,5},{7,6},{8,11},{9,8},{10,9... | collective-permute-start | bytes 196616 | tf_op jit(solution)/shard_map/ppermute | solution.py:489
  88.5 6.4 %collective-permute-start.3 = (f32[4,4,8,128]{3,2,1,0:T(8,128)}, f32[4,4,8,128]{3,2,1,0:T(8,128)S(1)}, u32[]{:S(2)}, u32[]{:S(2)}) collective-permute-start(f32[4,4,8,128]{3,2,1,0:T(8,128)} %get-tuple-element.15), channel_id=1, source_target_pairs={{0,2},{1,3},{2,0},{3,1},{4,6},{5,7},{6,4},{7,5},{8,10},{9,11},{10,... | collective-permute-start | bytes 196616 | tf_op jit(solution)/shard_map/ppermute | solution.py:489
  91.0 4.5 %collective-permute-start.2 = (f32[4,4,8,128]{3,2,1,0:T(8,128)}, f32[4,4,8,128]{3,2,1,0:T(8,128)S(1)}, u32[]{:S(2)}, u32[]{:S(2)}) collective-permute-start(f32[4,4,8,128]{3,2,1,0:T(8,128)} %get-tuple-element.15), channel_id=1, source_target_pairs={{0,1},{1,2},{2,3},{3,0},{4,5},{5,6},{6,7},{7,4},{8,9},{9,10},{10,1... | collective-permute-start | bytes 196616 | tf_op jit(solution)/shard_map/ppermute | solution.py:489
  96.5 27.6 %copy-start.4 = (bf16[2,768,256]{2,1,0:T(8,128)(2,1)S(1)}, bf16[2,768,256]{2,1,0:T(8,128)(2,1)}, u32[]{:S(2)}) copy-start(bf16[2,768,256]{2,1,0:T(8,128)(2,1)} %constant.46.clone.t_hbm) | copy-start | bytes 2359300
  124.1 8.9 %copy-start.2 = (f32[128,4,8,128]{3,2,1,0:T(8,128)S(1)}, f32[128,4,8,128]{3,2,1,0:T(8,128)}, u32[]{:S(2)}) copy-start(f32[128,4,8,128]{3,2,1,0:T(8,128)} %get-tuple-element.22.inv_hbm) | copy-start | bytes 6291460
  124.1 8.9 %copy-start.5 = (f32[128]{0:T(128)S(1)}, f32[128]{0:T(128)}, u32[]{:S(2)}) copy-start(f32[128]{0:T(128)} %get-tuple-element.29.up_ref) | copy-start | bytes 1540
  124.1 8.9 %copy-start.6 = (f32[128]{0:T(128)S(1)}, f32[128]{0:T(128)}, u32[]{:S(2)}) copy-start(f32[128]{0:T(128)} %get-tuple-element.30.low_ref) | copy-start | bytes 1540
  128.0 9.2 %collective-permute-start.7 = (f32[2,4,8,128]{3,2,1,0:T(8,128)S(1)}, f32[2,4,8,128]{3,2,1,0:T(8,128)S(1)}, u32[]{:S(2)}, u32[]{:S(2)}) collective-permute-start(f32[2,4,8,128]{3,2,1,0:T(8,128)S(1)} %get-tuple-element.23.refs_0_), channel_id=1, source_target_pairs={{0,3},{1,0},{2,1},{3,2},{4,7},{5,4},{6,5},{7,6},{8,11},{9,8},{10,9... | collective-permute-start | bytes 98312 | tf_op jit(solution)/shard_map/ppermute | solution.py:530
  128.6 8.7 %collective-permute-start.6 = (f32[2,4,8,128]{3,2,1,0:T(8,128)S(1)}, f32[2,4,8,128]{3,2,1,0:T(8,128)S(1)}, u32[]{:S(2)}, u32[]{:S(2)}) collective-permute-start(f32[2,4,8,128]{3,2,1,0:T(8,128)S(1)} %get-tuple-element.23.refs_0_), channel_id=1, source_target_pairs={{0,2},{1,3},{2,0},{3,1},{4,6},{5,7},{6,4},{7,5},{8,10},{9,11},{10,... | collective-permute-start | bytes 98312 | tf_op jit(solution)/shard_map/ppermute | solution.py:530
  131.1 6.1 %collective-permute-start.5 = (f32[2,4,8,128]{3,2,1,0:T(8,128)S(1)}, f32[2,4,8,128]{3,2,1,0:T(8,128)S(1)}, u32[]{:S(2)}, u32[]{:S(2)}) collective-permute-start(f32[2,4,8,128]{3,2,1,0:T(8,128)S(1)} %get-tuple-element.23.refs_0_), channel_id=1, source_target_pairs={{0,1},{1,2},{2,3},{3,0},{4,5},{5,6},{6,7},{7,4},{8,9},{9,10},{10,1... | collective-permute-start | bytes 98312 | tf_op jit(solution)/shard_map/ppermute | solution.py:530
  133.0 4.3 %copy-start = (f32[4,1024,128]{2,1,0:T(8,128)S(1)}, f32[4,1024,128]{2,1,0:T(8,128)}, u32[]{:S(2)}) copy-start(f32[4,1024,128]{2,1,0:T(8,128)} %get-tuple-element.19.v_hbm.refs_5_) | copy-start | bytes 6291460
  133.0 4.3 %copy-start.1 = (f32[4,1024,128]{2,1,0:T(8,128)S(1)}, f32[4,1024,128]{2,1,0:T(8,128)}, u32[]{:S(2)}) copy-start(f32[4,1024,128]{2,1,0:T(8,128)} %get-tuple-element.20.w_hbm.refs_6_) | copy-start | bytes 6291460
  133.1 4.3 %copy-start.3 = (bf16[2,256,768]{2,1,0:T(8,128)(2,1)S(1)}, bf16[2,256,768]{2,1,0:T(8,128)(2,1)}, u32[]{:S(2)}) copy-start(bf16[2,256,768]{2,1,0:T(8,128)(2,1)} %constant.47.clone.refs_7_.t_ref) | copy-start | bytes 2359300
